TPU v7x, 32 devices: a whole 2x2x4 slice. The times are simulated.
32 devices in a mesh: dp: 8 (over z, x), mp: 4 (over y, core).
Axes of the slice: x: 2, y: 2, z: 4, core: 2. Of those that a mesh axis runs over, the one named last changes fastest.
Arguments:
- layer_input: bfloat16 [16384, 768], P(('dp', 'mp')), may hold values from -6 to 6
- lengths: int32 [8, 8], P('dp'), may hold values from 1 to 1024, 2048 in all within a row
- key_mask: int32 [16384], P('dp'), may hold values 0 or 1
- input_gain: float32 [768], replicated, may hold values from 0.5 to 1.5
- input_bias: float32 [768], replicated, may hold values from -3 to 3
- qkv_weight: bfloat16 [768, 3, 768], P('dp', None, 'mp'), may hold values from -0.21875 to 0.21875
- mixed_gain: float32 [768], P('mp'), may hold values from 0.5 to 1.5
- mixed_bias: float32 [768], P('mp'), may hold values from -3 to 3
- out_weight: bfloat16 [768, 768], P('mp', 'dp'), may hold values from -0.21875 to 0.21875
- ffn_gain: float32 [768], replicated, may hold values from 0.5 to 1.5
- ffn_bias: float32 [768], replicated, may hold values from -3 to 3
- fc1_weight: bfloat16 [768, 3072], P('dp', 'mp'), may hold values from -0.21875 to 0.21875
- fc1_bias: float32 [3072], P('mp'), may hold values from -3 to 3
- hidden_gain: float32 [3072], P('mp'), may hold values from 0.5 to 1.5
- hidden_bias: float32 [3072], P('mp'), may hold values from -3 to 3
- fc2_weight: bfloat16 [3072, 768], P('mp', 'dp'), may hold values from -0.109375 to 0.109375
- out_grad: bfloat16 [16384, 768], P(('dp', 'mp')), may hold values from -6 to 6
Outputs:
- layer_output: bfloat16 [16384, 768], P(('dp', 'mp'))
- input_grad: float32 [16384, 768], P(('dp', 'mp'))
- input_gain_grad: float32 [768], replicated
- input_bias_grad: float32 [768], replicated
- qkv_grad: float32 [768, 3, 768], P('dp', None, 'mp')
- mixed_gain_grad: float32 [768], replicated
- mixed_bias_grad: float32 [768], replicated
- out_weight_grad: float32 [768, 768], P('mp', 'dp')
- ffn_gain_grad: float32 [768], replicated
- ffn_bias_grad: float32 [768], replicated
- fc1_grad: float32 [768, 3072], P('dp', 'mp')
- fc1_bias_grad: float32 [3072], replicated
- hidden_gain_grad: float32 [3072], replicated
- hidden_bias_grad: float32 [3072], replicated
- fc2_grad: float32 [3072, 768], P('mp', 'dp')
Inputs may be any that keep to these rules, and one draw needn't show every extreme that they name: Each row holds the lengths of 8 sequences packed in order into one group; a row sums to 2048 and its largest entry is exactly 1024.
All inputs are finite; a program needn't handle non-finite values. No bound on the sum of `key_mask` on one device may be relied on, other than what follows from the above.
Results may differ from a plain program's by a relative error of at most 0.012.
Values may be sent and summed in bfloat16 or wider, within the bound.
No kernel may reach another device: no remote copies, remote signals or barrier semaphores. Data moves between devices by JAX's collectives and lax.ppermute only.
A program may use at most 128 MiB of HBM per device.

v0:
```python
from functools import partial

import jax
import jax.numpy as jnp
from jax import lax
from jax.sharding import PartitionSpec as P

D = 768
HEAD_DIM = 64
FF = 3072


EPS = 1e-05


def segment_ids(length_row, length_all):
    seq_ends = jnp.cumsum(length_row)
    places = jnp.arange(length_all, dtype=jnp.int32)
    return jnp.sum((places[:, None] >= seq_ends[None, :]).astype(jnp.int32), axis=1)


def local_norm(values, norm_gain, norm_bias):
    row_mean = jnp.mean(values, axis=-1, keepdims=True)
    centred = values - row_mean
    row_var = jnp.mean(centred * centred, axis=-1, keepdims=True)
    inv_std = lax.rsqrt(row_var + EPS)
    normed = centred * inv_std
    return (normed * norm_gain + norm_bias, normed, inv_std)


def local_norm_back(gradient, normed, inv_std, norm_gain):
    scaled = gradient * norm_gain
    primary = jnp.mean(scaled, axis=-1, keepdims=True)
    second = jnp.mean(scaled * normed, axis=-1, keepdims=True)
    return (
        inv_std * (scaled - primary - normed * second),
        jnp.sum(gradient * normed, axis=0),
        jnp.sum(gradient, axis=0),
    )


def stat_one(values):
    return lax.psum(values, "mp")


def stat_pair(primary, second):
    return lax.psum((primary, second), "mp")


def split_norm(values, norm_gain, norm_bias, full_width):
    row_mean = stat_one(jnp.sum(values, axis=1)) / full_width
    centred = values - row_mean[:, None]
    row_var = stat_one(jnp.sum(centred * centred, axis=1)) / full_width
    inv_std = lax.rsqrt(row_var + EPS)[:, None]
    normed = centred * inv_std
    return (normed * norm_gain + norm_bias, normed, inv_std)


def split_norm_back(gradient, normed, inv_std, norm_gain, full_width):
    scaled = gradient * norm_gain
    primary, second = stat_pair(jnp.sum(scaled, axis=1), jnp.sum(scaled * normed, axis=1))
    result = inv_std * (
        scaled - primary[:, None] / full_width - normed * second[:, None] / full_width
    )
    return (result, jnp.sum(gradient * normed, axis=0), jnp.sum(gradient, axis=0))


def mask_block(segment, key_keep, first_row, block_rows):
    columns = jnp.arange(segment.shape[0], dtype=jnp.int32)
    row_ids = first_row + jnp.arange(block_rows, dtype=jnp.int32)
    seg_rows = lax.dynamic_slice_in_dim(segment, first_row, block_rows, 0)
    return (seg_rows[:, None] == segment[None, :]) & (
        (key_keep[None, :] == 1) | (row_ids[:, None] == columns[None, :])
    )


def block_scores(block_q, key_mat, allowed, score_scale):
    scores = (
        jnp.einsum("qhe,khe->hqk", block_q, key_mat, preferred_element_type=jnp.float32)
        * score_scale
    )
    return jnp.where(allowed[None], scores, -1e30)


def attend_forward(queries, key_mat, value_mat, segment, key_keep, score_scale):
    length_all, head_count, head_size = queries.shape
    block_rows = min(512, length_all)
    blocks = length_all // block_rows

    def one_block(inputs):
        block_q, first_row = inputs
        scores = block_scores(
            block_q, key_mat, mask_block(segment, key_keep, first_row, block_rows), score_scale
        )
        row_max = jnp.max(scores, axis=-1, keepdims=True)
        exp_scores = jnp.exp(scores - row_max)
        row_total = jnp.sum(exp_scores, axis=-1, keepdims=True)
        probabilities = (exp_scores / row_total).astype(jnp.bfloat16)
        result = jnp.einsum(
            "hqk,khe->qhe", probabilities, value_mat, preferred_element_type=jnp.float32
        )
        return (result, (row_max + jnp.log(row_total))[..., 0])

    starts = jnp.arange(blocks, dtype=jnp.int32) * block_rows
    result, log_total = lax.map(
        one_block, (queries.reshape(blocks, block_rows, head_count, head_size), starts)
    )
    return (result.reshape(length_all, head_count * head_size), log_total)


def attend_backward(
    queries, key_mat, value_mat, segment, key_keep, score_scale, log_total, grad_att
):
    length_all, head_count, head_size = queries.shape
    block_rows = min(512, length_all)
    blocks = length_all // block_rows

    def one_block(carried, inputs):
        grad_key, grad_value = carried
        block_q, block_g, block_log, first_row = inputs
        scores = block_scores(
            block_q, key_mat, mask_block(segment, key_keep, first_row, block_rows), score_scale
        )
        probabilities = jnp.exp(scores - block_log[..., None])
        grad_probs = jnp.einsum(
            "qhe,khe->hqk", block_g, value_mat, preferred_element_type=jnp.float32
        )
        row_dot = jnp.sum(probabilities * grad_probs, axis=-1, keepdims=True)
        grad_scores = (probabilities * (grad_probs - row_dot)).astype(jnp.bfloat16)
        grad_query = (
            jnp.einsum("hqk,khe->qhe", grad_scores, key_mat, preferred_element_type=jnp.float32)
            * score_scale
        )
        grad_key = (
            grad_key
            + jnp.einsum("hqk,qhe->khe", grad_scores, block_q, preferred_element_type=jnp.float32)
            * score_scale
        )
        grad_value = grad_value + jnp.einsum(
            "hqk,qhe->khe",
            probabilities.astype(jnp.bfloat16),
            block_g,
            preferred_element_type=jnp.float32,
        )
        return ((grad_key, grad_value), grad_query)

    zeros_kv = jnp.zeros((length_all, head_count, head_size), jnp.float32)
    starts = jnp.arange(blocks, dtype=jnp.int32) * block_rows
    shape_blocks = (blocks, block_rows, head_count, head_size)
    (grad_key, grad_value), grad_query = lax.scan(
        one_block,
        (zeros_kv, zeros_kv),
        (queries.reshape(shape_blocks), grad_att.reshape(shape_blocks), log_total, starts),
    )
    flat = (length_all, head_count * head_size)
    return (grad_query.reshape(flat), grad_key.reshape(flat), grad_value.reshape(flat))


def contract_first(left, right):
    return lax.dot_general(
        left, right, (((0,), (0,)), ((), ())), preferred_element_type=jnp.float32
    )


def contract_last(left, right):
    return lax.dot_general(
        left, right, (((1,), (1,)), ((), ())), preferred_element_type=jnp.float32
    )


def per_device(
    layer_input,
    lengths,
    key_mask,
    input_gain,
    input_bias,
    qkv_weight,
    mixed_gain,
    mixed_bias,
    out_weight,
    ffn_gain,
    ffn_bias,
    fc1_weight,
    fc1_bias,
    hidden_gain,
    hidden_bias,
    fc2_weight,
    out_grad,
):
    row_count = layer_input.shape[0]
    mp_index = lax.axis_index("mp")
    score_scale = HEAD_DIM ** (-0.5)
    segment = segment_ids(lengths[0], key_mask.shape[0])

    def full_rows(values):
        return lax.all_gather(values, "mp", axis=0, tiled=True)

    def reduce_rows(product):
        return lax.psum_scatter(
            product(jnp.int32(0), lax.axis_size("mp") * row_count),
            "mp",
            scatter_dimension=0,
            tiled=True,
        )

    qkv_full, out_full, fc1_full, fc2_full = (
        lax.all_gather(qkv_weight, "dp", axis=0, tiled=True),
        lax.all_gather(out_weight, "dp", axis=1, tiled=True),
        lax.all_gather(fc1_weight, "dp", axis=0, tiled=True),
        lax.all_gather(fc2_weight, "dp", axis=1, tiled=True),
    )
    input_f = layer_input.astype(jnp.float32)
    normed_in, unit_in, inv_in = local_norm(input_f, input_gain, input_bias)
    lowered_in = full_rows(normed_in.astype(jnp.bfloat16))
    projected = jnp.einsum(
        "td,dcf->tcf", lowered_in, qkv_full, preferred_element_type=jnp.float32
    ).astype(jnp.bfloat16)
    group_len = projected.shape[0]
    head_count = projected.shape[2] // HEAD_DIM
    head_shape = (group_len, head_count, HEAD_DIM)
    queries = projected[:, 0].reshape(head_shape)
    key_mat = projected[:, 1].reshape(head_shape)
    value_mat = projected[:, 2].reshape(head_shape)
    attended, log_total = attend_forward(
        queries, key_mat, value_mat, segment, key_mask, score_scale
    )
    normed_mix, unit_mix, inv_mix = split_norm(attended, mixed_gain, mixed_bias, D)
    lowered_mix = normed_mix.astype(jnp.bfloat16)

    def mix_product(first_row, span):
        return jnp.dot(lowered_mix, out_full, preferred_element_type=jnp.float32)

    residual = input_f + reduce_rows(mix_product)
    normed_ffn, unit_ffn, inv_ffn = local_norm(residual, ffn_gain, ffn_bias)
    lowered_ffn = full_rows(normed_ffn.astype(jnp.bfloat16))
    pre_act = jnp.dot(lowered_ffn, fc1_full, preferred_element_type=jnp.float32) + fc1_bias
    gelu_exact = partial(jax.nn.gelu, approximate=False)
    activated, gelu_back = jax.vjp(gelu_exact, pre_act)
    normed_hid, unit_hid, inv_hid = split_norm(activated, hidden_gain, hidden_bias, FF)
    lowered_hid = normed_hid.astype(jnp.bfloat16)

    def hid_product(first_row, span):
        return jnp.dot(
            lax.dynamic_slice_in_dim(lowered_hid, first_row, span, 0),
            fc2_full,
            preferred_element_type=jnp.float32,
        )

    layer_output = (residual + reduce_rows(hid_product)).astype(jnp.bfloat16)
    qkv_full, out_full, fc1_full, fc2_full = (
        lax.all_gather(qkv_weight, "dp", axis=0, tiled=True),
        lax.all_gather(out_weight, "dp", axis=1, tiled=True),
        lax.all_gather(fc1_weight, "dp", axis=0, tiled=True),
        lax.all_gather(fc2_weight, "dp", axis=1, tiled=True),
    )
    grad_rows = full_rows(out_grad)
    fc2_grad = contract_first(lowered_hid, grad_rows)
    grad_hid = contract_last(grad_rows, fc2_full)
    grad_act, hidden_gain_grad, hidden_bias_grad = split_norm_back(
        grad_hid, unit_hid, inv_hid, hidden_gain, FF
    )
    grad_pre = gelu_back(grad_act)[0].astype(jnp.bfloat16)
    fc1_bias_grad = jnp.sum(grad_pre.astype(jnp.float32), axis=0)
    fc1_grad = contract_first(lowered_ffn, grad_pre)

    def ffn_back(first_row, span):
        return contract_last(grad_pre, fc1_full)

    grad_ffn_in, ffn_gain_grad, ffn_bias_grad = local_norm_back(
        reduce_rows(ffn_back), unit_ffn, inv_ffn, ffn_gain
    )
    grad_resid = out_grad.astype(jnp.float32) + grad_ffn_in
    grad_mix_rows = full_rows(grad_resid.astype(jnp.bfloat16))
    out_weight_grad = contract_first(lowered_mix, grad_mix_rows)
    grad_mix = contract_last(grad_mix_rows, out_full)
    grad_att, mixed_gain_grad, mixed_bias_grad = split_norm_back(
        grad_mix, unit_mix, inv_mix, mixed_gain, D
    )
    grad_query, grad_key, grad_value = attend_backward(
        queries,
        key_mat,
        value_mat,
        segment,
        key_mask,
        score_scale,
        log_total,
        grad_att.astype(jnp.bfloat16).reshape(head_shape),
    )
    grad_proj = jnp.stack([grad_query, grad_key, grad_value], axis=1).astype(jnp.bfloat16)
    qkv_grad = jnp.einsum("td,tcf->dcf", lowered_in, grad_proj, preferred_element_type=jnp.float32)

    def input_back(first_row, span):
        return jnp.einsum("tcf,dcf->td", grad_proj, qkv_full, preferred_element_type=jnp.float32)

    grad_in, input_gain_grad, input_bias_grad = local_norm_back(
        reduce_rows(input_back), unit_in, inv_in, input_gain
    )
    input_grad = grad_resid + grad_in
    qkv_grad, out_weight_grad, fc1_grad, fc2_grad = (
        lax.psum_scatter(qkv_grad, "dp", scatter_dimension=0, tiled=True),
        lax.psum_scatter(out_weight_grad, "dp", scatter_dimension=1, tiled=True),
        lax.psum_scatter(fc1_grad, "dp", scatter_dimension=0, tiled=True),
        lax.psum_scatter(fc2_grad, "dp", scatter_dimension=1, tiled=True),
    )

    def placed(vector, full_width):
        return lax.dynamic_update_slice_in_dim(
            jnp.zeros((full_width,), jnp.float32), vector, mp_index * vector.shape[0], 0
        )

    summed = lax.psum(
        (
            input_gain_grad,
            input_bias_grad,
            placed(mixed_gain_grad, D),
            placed(mixed_bias_grad, D),
            ffn_gain_grad,
            ffn_bias_grad,
            placed(fc1_bias_grad, FF),
            placed(hidden_gain_grad, FF),
            placed(hidden_bias_grad, FF),
        ),
        ("dp", "mp"),
    )
    return (
        layer_output,
        input_grad,
        summed[0],
        summed[1],
        qkv_grad,
        summed[2],
        summed[3],
        out_weight_grad,
        summed[4],
        summed[5],
        fc1_grad,
        summed[6],
        summed[7],
        summed[8],
        fc2_grad,
    )


def solution(mesh):
    return jax.shard_map(
        per_device,
        mesh=mesh,
        in_specs=(
            P(("dp", "mp"), None),
            P("dp", None),
            P("dp"),
            P(),
            P(),
            P("dp", None, "mp"),
            P("mp"),
            P("mp"),
            P("mp", "dp"),
            P(),
            P(),
            P("dp", "mp"),
            P("mp"),
            P("mp"),
            P("mp"),
            P("mp", "dp"),
            P(("dp", "mp"), None),
        ),
        out_specs=(
            P(("dp", "mp"), None),
            P(("dp", "mp"), None),
            P(),
            P(),
            P("dp", None, "mp"),
            P(),
            P(),
            P("mp", "dp"),
            P(),
            P(),
            P("dp", "mp"),
            P(),
            P(),
            P(),
            P("mp", "dp"),
        ),
        check_vma=False,
    )
```

profile of v0, /device:TPU:0, one launch (start us, length us, event | category | flops | bytes accessed | tf_op | source)
XLA Modules:
  0.0 1092.5 jit_solution(16780625240244555772)
XLA Ops:
  15.1 39.1 %all_gather.29 = bf16[768,3,192]{2,1,0:T(4,128)(2,1)S(1)} all-gather(bf16[96,3,192]{2,1,0:T(4,128)(2,1)S(1)} %copy.54), channel_id=1, replica_groups=mesh['dp'=8,'mp'=4] {'dp'}, dimensions={0}, use_global_device_ids=true | all-gather | bytes 995328 | tf_op jit(solution)/shard_map/all_gather | solution.py:207
  56.8 31.4 %all_gather.30 = bf16[192,768]{0,1:T(8,128)(2,1)S(1)} all-gather(bf16[192,96]{0,1:T(8,128)(2,1)} %copy.58), channel_id=1, replica_groups=mesh['dp'=8,'mp'=4] {'dp'}, dimensions={1}, use_global_device_ids=true | all-gather | bytes 331776 | tf_op jit(solution)/shard_map/all_gather | solution.py:208
  99.0 105.2 %while.29 = (s32[]{:T(128)}, f32[4,512,3,64]{1,3,2,0:T(8,128)S(1)}, f32[4,3,512]{2,1,0:T(4,128)}, s32[4]{0:T(128)}, s32[2048]{0:T(1024)S(1)}, /*index=5*/s32[204...) while((s32[]{:T(128)}, f32[4,512,3,64]{1,3,2,0:T(8,128)S(1)}, ...), condition=%wide.region_7.8_spmd.clone, body=%wide.region_4.7_spmd.sunk.clone | while | flops 847250432 | bytes 44191908 | solution.py:105
  104.4 6.8 fusion.150
  130.7 6.8 fusion.150
  137.5 6.8 fusion.151
  157.0 6.8 fusion.150
  183.2 6.8 fusion.150
  190.1 6.8 fusion.151
  221.0 7.6 psum.120
  236.3 55.5 %reduce-scatter.11.cloned.1.call-done = f32[512,768]{1,0:T(8,128)} async-done(((f32[2048,768]{1,0:T(8,128)}), f32[512,768]{1,0:T(8,128)}) %reduce-scatter.11.cloned.1.call-update) | async-done | bytes 1572880 | tf_op jit(solution)/shard_map/reduce_scatter | solution.py:199
  296.8 11.4 %all-gather.15.cloned.1.call-done = bf16[2048,768]{1,0:T(8,128)(2,1)} async-done(((bf16[512,768]{1,0:T(8,128)(2,1)}), bf16[2048,768]{1,0:T(8,128)(2,1)}) %all-gather.15.cloned.1.call-update) | async-done | bytes 3145744 | tf_op jit(solution)/shard_map/all_gather | solution.py:196
  308.2 8.1 fusion.75
  323.0 28.9 %all-gather.11.cloned.1.call-done = bf16[768,768]{1,0:T(8,128)(2,1)} async-done(((bf16[96,768]{1,0:T(8,128)(2,1)}), bf16[768,768]{1,0:T(8,128)(2,1)}) %all-gather.11.cloned.1.call-update) | async-done | bytes 1179664 | tf_op jit(solution)/shard_map/all_gather | solution.py:209
  351.8 29.1 %all-gather.9.cloned.1.call-done = bf16[2048,768]{1,0:T(8,128)(2,1)} async-done(((bf16[512,768]{1,0:T(8,128)(2,1)}), bf16[2048,768]{1,0:T(8,128)(2,1)}) %all-gather.9.cloned.1.call-update) | async-done | bytes 3145744 | tf_op jit(solution)/shard_map/all_gather | solution.py:196
  381.0 21.7 %fusion.71 = (f32[2048]{0:T(1024)}, f32[2048,768]{0,1:T(8,128)}, f32[2048,768]{0,1:T(8,128)}, f32[2048,768]{0,1:T(8,128)}) fusion(f32[768]{0:T(1024)} %param.33, bf16[2048,768]{1,0:T(8,128)(2,1)} %all-gather.9.cloned.1.call-done, bf16[768,768]{1,0:T(8,128)(2,1)} %all-gather.11.cloned.1.call-done), kind=kOutput, calls=%fused_computation.139 | convolution fusion | flops 2519726080 | bytes 23211008 | tf_op jit(solution)/shard_map/dot_general | solution.py:236
  414.7 16.7 %psum.122 = f32[2048]{0:T(1024)} all-reduce(f32[2048]{0:T(1024)} %multiply_reduce_fusion.3), channel_id=1, replica_groups=mesh['dp'=8,'mp'=4] {'mp'}, use_global_device_ids=true, to_apply=%region_18.19 | all-reduce | flops 2048 | bytes 16384 | tf_op jit(solution)/shard_map/psum | solution.py:43
  438.6 12.3 %all-reduce.2 = (f32[2048]{0:T(1024)}, f32[2048]{0:T(1024)}) all-reduce(f32[2048]{0:T(1024)} %get-tuple-element.235, f32[2048]{0:T(1024)} %get-tuple-element.236), channel_id=1, replica_groups=mesh['dp'=8,'mp'=4] {'mp'}, use_global_device_ids=true, to_apply=%region_23.24 | all-reduce | flops 4096 | bytes 32768 | tf_op jit(solution)/shard_map/psum | solution.py:47
  451.6 13.4 %convert_reduce_fusion = (f32[768]{0:T(1024)}, bf16[2048,768]{0,1:T(8,128)(2,1)S(1)}, bf16[2048,768]{0,1:T(8,128)(2,1)}) fusion(f32[2048,768]{0,1:T(8,128)} %get-tuple-element.310, f32[2048]{0:T(1024)} %get-tuple-element.302, f32[2048,768]{0,1:T(8,128)} %get-tuple-element.309, f32[2048]{0:T(1024)} %copy-done.22, f32[2048]{0:T(1024)S(1)} %broadcast_multiply_fusion, ...), kind=kLoop, calls=%fused_computation.59 | loop fusion | flops 44039424 | bytes 31502336 | tf_op jit(solution)/shard_map/reduce_sum | solution.py:263
  471.5 8.3 fusion.77
  479.8 50.3 %reduce-scatter.15.cloned.1.call-done = f32[512,768]{1,0:T(8,128)} async-done(((f32[2048,768]{1,0:T(8,128)}), f32[512,768]{1,0:T(8,128)}) %reduce-scatter.15.cloned.1.call-update) | async-done | bytes 1572880 | tf_op jit(solution)/shard_map/reduce_scatter | solution.py:199
  533.4 57.5 %reduce-scatter.13.cloned.1.call-done = f32[512,768]{1,0:T(8,128)} async-done(((f32[2048,768]{1,0:T(8,128)}), f32[512,768]{1,0:T(8,128)}) %reduce-scatter.13.cloned.1.call-update) | async-done | bytes 1572880 | tf_op jit(solution)/shard_map/reduce_scatter | solution.py:199
  596.5 27.6 %all-gather.17.cloned.1.call-done = bf16[2048,768]{1,0:T(8,128)(2,1)} async-done(((bf16[512,768]{1,0:T(8,128)(2,1)}), bf16[2048,768]{1,0:T(8,128)(2,1)}) %all-gather.17.cloned.1.call-update) | async-done | bytes 3145744 | tf_op jit(solution)/shard_map/all_gather | solution.py:196
  634.0 11.3 %all-reduce.1 = (f32[2048]{0:T(1024)S(1)}, f32[2048]{0:T(1024)S(1)}) all-reduce(f32[2048]{0:T(1024)} %get-tuple-element.238, f32[2048]{0:T(1024)} %get-tuple-element.245), channel_id=1, replica_groups=mesh['dp'=8,'mp'=4] {'mp'}, use_global_device_ids=true, to_apply=%region_30.31 | all-reduce | flops 4096 | bytes 32768 | tf_op jit(solution)/shard_map/psum | solution.py:47
  650.6 145.4 %while.30 = (s32[]{:T(128)}, f32[2048,3,64]{0,2,1:T(8,128)}, f32[2048,3,64]{0,2,1:T(8,128)}, bf16[4,512,3,64]{1,3,2,0:T(8,128)(2,1)}, bf16[4,512,3,64]{1,3,2,0:T...) while((s32[]{:T(128)}, f32[2048,3,64]{0,2,1:T(8,128)}, ...), condition=%wide.region_33.34_spmd.clone.clone, body=%wide.region_31.33_spmd.clone.sunk.clone | while | flops 2066711552 | bytes 156707280 | solution.py:150
  806.9 7.2 fusion.79
  820.5 6.9 fusion.51
  830.7 35.4 %reduce-scatter.17.cloned.1.call-done = f32[512,768]{1,0:T(8,128)} async-done(((f32[2048,768]{1,0:T(8,128)}), f32[512,768]{1,0:T(8,128)}) %reduce-scatter.17.cloned.1.call-update) | async-done | bytes 1572880 | tf_op jit(solution)/shard_map/reduce_scatter | solution.py:199
  868.4 42.5 %all-reduce = (f32[768]{0:T(1024)}, f32[768]{0:T(1024)}, f32[768]{0:T(1024)}, f32[768]{0:T(1024)}, f32[768]{0:T(1024)}, /*index=5*/f32[768]{0:T(1024)}, f32[3072]{0:T(1024)}, f32[3072]{0:T(1024)}, f32[3072]{0:T(1024)}) all-reduce(f32[768]{0:T(1024)S(1)} %get-tuple-element.241, ...), channel_id=1, replica_groups=mesh['dp'=8,'mp'=4] {'dp','mp'}, use_global_device_ids=true, to_apply=%region_38.39 | all-reduce | flops 13824 | bytes 110592 | tf_op jit(solution)/shard_map/psum | solution.py:311
  914.0 26.1 %reduce-scatter.21.cloned.1.call-done = f32[96,768]{1,0:T(8,128)} async-done(((f32[768,768]{1,0:T(8,128)}), f32[96,768]{1,0:T(8,128)}) %reduce-scatter.21.cloned.1.call-update) | async-done | bytes 294928 | tf_op jit(solution)/shard_map/reduce_scatter | solution.py:302
  940.1 72.6 %reduce-scatter.23.cloned.1.call-done = f32[768,96]{0,1:T(8,128)} async-done(((f32[768,768]{0,1:T(8,128)}), f32[768,96]{0,1:T(8,128)}) %reduce-scatter.23.cloned.1.call-update) | async-done | bytes 294928 | tf_op jit(solution)/shard_map/reduce_scatter | solution.py:303
  1012.7 72.3 %reduce-scatter.19.cloned.1.call-done = f32[96,3,192]{2,0,1:T(8,128)} async-done(((f32[768,3,192]{2,0,1:T(8,128)}), f32[96,3,192]{2,0,1:T(8,128)}) %reduce-scatter.19.cloned.1.call-update) | async-done | bytes 221200 | tf_op jit(solution)/shard_map/reduce_scatter | solution.py:300
  (316 shorter events, 325.2 us)
Async XLA Ops:
  8.0 80.2 %all-gather.7.cloned.1.call-start = ((), (), s32[]{:S(2)}) async-start(), calls=%async_computation.8 | async-start | bytes 3932160 | tf_op jit(solution)/shard_map/all_gather | solution.py:196
  14.0 277.8 %reduce-scatter.11.cloned.1.call-start = ((), (), s32[]{:S(2)}) async-start(), calls=%async_computation.9 | async-start | bytes 7864320 | tf_op jit(solution)/shard_map/reduce_scatter | solution.py:199
  220.3 14.1 %copy-start.8 = (f32[24,8,4,512]{3,1,2,0:T(8,128)}, f32[24,8,4,512]{3,1,2,0:T(8,128)S(1)}, u32[]{:S(2)}) copy-start(f32[24,8,4,512]{3,1,2,0:T(8,128)S(1)} %copy.70) | copy-start | bytes 4718596
  234.5 62.3 %all-gather.13.cloned.1.call-start = ((), (), s32[]{:S(2)}) async-start(), calls=%async_computation.12 | async-start | bytes 1327104 | tf_op jit(solution)/shard_map/all_gather | solution.py:210
  235.1 73.2 %all-gather.15.cloned.1.call-start = ((), (), s32[]{:S(2)}) async-start(), calls=%async_computation.14 | async-start | bytes 3932160 | tf_op jit(solution)/shard_map/all_gather | solution.py:196
  235.6 116.2 %all-gather.11.cloned.1.call-start = ((), (), s32[]{:S(2)}) async-start(), calls=%async_computation.11 | async-start | bytes 1327104 | tf_op jit(solution)/shard_map/all_gather | solution.py:209
  236.2 144.7 %all-gather.9.cloned.1.call-start = ((), (), s32[]{:S(2)}) async-start(), calls=%async_computation.10 | async-start | bytes 3932160 | tf_op jit(solution)/shard_map/all_gather | solution.py:196
  296.7 233.4 %reduce-scatter.15.cloned.1.call-start = ((), (), s32[]{:S(2)}) async-start(), calls=%async_computation.15 | async-start | bytes 7864320 | tf_op jit(solution)/shard_map/reduce_scatter | solution.py:199
  451.6 15.1 %copy-start.39 = (bf16[768,768]{1,0:T(8,128)(2,1)S(1)}, bf16[768,768]{1,0:T(8,128)(2,1)}, u32[]{:S(2)}) copy-start(bf16[768,768]{1,0:T(8,128)(2,1)} %all-gather.11.cloned.1.call-done) | copy-start | bytes 3538948
  471.4 119.5 %reduce-scatter.13.cloned.1.call-start = ((), (), s32[]{:S(2)}) async-start(), calls=%async_computation.13 | async-start | bytes 7864320 | tf_op jit(solution)/shard_map/reduce_scatter | solution.py:199
  479.8 144.4 %all-gather.17.cloned.1.call-start = ((), (), s32[]{:S(2)}) async-start(), calls=%async_computation.16 | async-start | bytes 3932160 | tf_op jit(solution)/shard_map/all_gather | solution.py:196
  595.5 233.6 %reduce-scatter.25.cloned.1.call-start = ((), (), s32[]{:S(2)}) async-start(), calls=%async_computation.21 | async-start | bytes 884736
  596.5 32.4 %copy-start.9 = (f32[24,8,4,512]{3,1,2,0:T(8,128)S(1)}, f32[24,8,4,512]{3,1,2,0:T(8,128)}, u32[]{:S(2)}) copy-start(f32[24,8,4,512]{3,1,2,0:T(8,128)} %copy-done.8) | copy-start | bytes 4718596
  628.9 237.2 %reduce-scatter.17.cloned.1.call-start = ((), (), s32[]{:S(2)}) async-start(), calls=%async_computation.17 | async-start | bytes 7864320 | tf_op jit(solution)/shard_map/reduce_scatter | solution.py:199
  651.0 8.6 copy-start.2
  651.0 8.6 copy-start.5
  722.4 8.6 copy-start.2
  722.4 8.6 copy-start.5
  722.5 8.6 copy-start.11
  759.1 8.6 copy-start.2
  759.1 8.6 copy-start.5
  759.1 8.6 copy-start.11
  806.9 133.3 %reduce-scatter.21.cloned.1.call-start = ((), (), s32[]{:S(2)}) async-start(), calls=%async_computation.19 | async-start | bytes 2654208 | tf_op jit(solution)/shard_map/reduce_scatter | solution.py:302
  814.2 198.5 %reduce-scatter.23.cloned.1.call-start = ((), (), s32[]{:S(2)}) async-start(), calls=%async_computation.20 | async-start | bytes 2654208 | tf_op jit(solution)/shard_map/reduce_scatter | solution.py:303
  820.4 45.7 %copy-start.25 = (f32[512]{0:T(512)S(1)}, f32[512]{0:T(512)}, u32[]{:S(2)}) copy-start(f32[512]{0:T(512)} %copy-done.24) | copy-start | bytes 6148
  820.4 45.7 %copy-start.28 = (f32[768]{0:T(1024)S(1)}, f32[768]{0:T(1024)}, u32[]{:S(2)}) copy-start(f32[768]{0:T(1024)} %param.24) | copy-start | bytes 9220
  820.4 45.7 %copy-start.30 = (f32[512]{0:T(512)S(1)}, f32[512]{0:T(512)}, u32[]{:S(2)}) copy-start(f32[512]{0:T(512)} %copy-done.29) | copy-start | bytes 6148
  820.5 264.5 %reduce-scatter.19.cloned.1.call-start = ((), (), s32[]{:S(2)}) async-start(), calls=%async_computation.18 | async-start | bytes 2654208 | tf_op jit(solution)/shard_map/reduce_scatter | solution.py:300
  827.4 38.8 %copy-start.7 = (bf16[512,768]{1,0:T(8,128)(2,1)S(1)}, bf16[512,768]{1,0:T(8,128)(2,1)}, u32[]{:S(2)}) copy-start(bf16[512,768]{1,0:T(8,128)(2,1)} %param.21) | copy-start | bytes 2359300
  827.4 41.0 %copy-start.34 = (f32[768]{0:T(1024)S(1)}, f32[768]{0:T(1024)}, u32[]{:S(2)}) copy-start(f32[768]{0:T(1024)} %get-tuple-element.239) | copy-start | bytes 9220
  827.4 41.0 %copy-start.35 = (f32[768]{0:T(1024)S(1)}, f32[768]{0:T(1024)}, u32[]{:S(2)}) copy-start(f32[768]{0:T(1024)} %get-tuple-element.246) | copy-start | bytes 9220
  827.4 83.5 %copy-start.10 = (f32[512,768]{1,0:T(8,128)S(1)}, f32[512,768]{1,0:T(8,128)}, u32[]{:S(2)}) copy-start(f32[512,768]{1,0:T(8,128)} %get-tuple-element.307) | copy-start | bytes 4718596
  (48 other events, 220.7 us)
Sparse Core Ops, SparseCore 0:
  14.1 31.2 all-gather.6
  234.6 57.1 reduce-scatter.10
  595.6 28.5 all-gather.16
Sparse Core Ops, SparseCore 1:
  237.1 39.8 all-gather.12
  278.5 29.7 all-gather.14
  310.3 41.5 all-gather.10
  354.1 26.8 all-gather.8
  471.5 58.6 reduce-scatter.14
  532.7 58.2 reduce-scatter.12
  629.0 62.5 reduce-scatter.24
  806.9 59.2 reduce-scatter.16
  870.5 69.6 reduce-scatter.20
  944.6 68.0 reduce-scatter.22
  1017.0 67.9 reduce-scatter.18
where the time goes:
time: 1100 us; the launch traced here: 1090 us
  waiting for transfers between devices  469 us (43%)
  matrix products  238 us (22%)
  blocking collectives  174 us (16%)
  other arithmetic  130 us (12%)
  local copies, waits for them, and re-layouts  48.7 us (4%)
  loops' own time  16.8 us (2%)
  between operations  16.2 us (1%)
    reduce_scatter x4, waiting for transfers between devices, reduce_rows(): lax.psum_scatter(product(jnp.int32(0), lax.axis_size('mp') * row_count),...  199 us
    reduce_scatter x1, waiting for transfers between devices, per_device(): lax.psum_scatter(fc2_grad, 'dp', scatter_dimension=1, tiled=True)  72.6 us
    reduce_scatter x1, waiting for transfers between devices, per_device(): lax.psum_scatter(qkv_grad, 'dp', scatter_dimension=0, tiled=True)  72.3 us
    all_gather x4, waiting for transfers between devices, full_rows(): return lax.all_gather(values, 'mp', axis=0, tiled=True)  68.2 us
    psum x1, blocking collectives, per_device(): lax.psum((input_gain_grad, input_bias_grad, placed(mixed_gain_grad, D), p...  42.5 us
    dot_general x8, matrix products, block_scores(): jnp.einsum('qhe,khe->hqk', block_q, key_mat, preferred_element_type=jnp.f...  39.3 us
    all_gather x1, blocking collectives, per_device(): lax.all_gather(qkv_weight, 'dp', axis=0, tiled=True)  39.1 us
    psum x4, blocking collectives, stat_one(): return lax.psum(values, 'mp')  37.5 us
  transfers between devices with their start and end apart: 14, of which 11 were waited for; matrix products, arithmetic and copies ran while one was open for 20% of the time, Pallas kernels for 0%

commit v1 on v0

v1 whole, which is shorter than its diff:
```python
import functools

import jax
import jax.numpy as jnp
from jax import lax
from jax.experimental import pallas as pl
from jax.experimental.pallas import tpu as pltpu
from jax.sharding import PartitionSpec as P

HD = 64
EPS = 1e-05
BIG = 1e30
NT = (((1,), (1,)), ((), ()))
NN = (((1,), (0,)), ((), ()))
TN = (((0,), (0,)), ((), ()))
bf16 = jnp.bfloat16
f32 = jnp.float32
VMEM_LIMIT = 56 * 2**20


def dot(a, b, dims=NN):
    return lax.dot_general(a, b, dims, preferred_element_type=f32)


def split3(x):
    high = x.astype(bf16).astype(f32)
    rest = x - high
    mid = rest.astype(bf16).astype(f32)
    return high, mid, rest - mid


def head_tile(ref, rows, col):
    at = col // 128 * 128
    width = min(128, ref.shape[-1] - at)
    x = ref[rows, at : at + width].astype(f32)
    if width < 128:
        x = jnp.concatenate([x, jnp.zeros((x.shape[0], 128 - width), f32)], axis=1)
    if col % 128:
        x = pltpu.roll(x, 64, 1)
    return x


def pack_heads(parts, low):
    tiles = []
    for i in range(0, len(parts), 2):
        if i + 1 < len(parts):
            tiles.append(jnp.where(low, parts[i], pltpu.roll(parts[i + 1], 64, 1)))
        else:
            tiles.append(parts[i][:, :64])
    return tiles


def seq_ends(len_ref, nseq):
    ends, total = [], jnp.int32(0)
    for j in range(nseq):
        total = total + len_ref[0, j]
        ends.append(total)
    return ends


def key_range(ends, first, last):
    lo, hi, start = jnp.int32(0), jnp.int32(0), jnp.int32(0)
    for end in ends:
        lo = jnp.where(first >= end, end, lo)
        hi = jnp.where(last >= start, end, hi)
        start = end
    return lo, hi


def fwd_kernel(m_ref, len_ref, mask_ref, qa_in, qb_in, o_ref, of_ref, qa, ka, va, *, heads, chunk, BQ, BK, nseq):
    G = qa.shape[1]
    nch, W = G // chunk, heads * HD
    half = nch // 2
    m = m_ref[0]
    ends = seq_ends(len_ref, nseq)
    lane = lax.broadcasted_iota(jnp.int32, (1, 128), 1)
    startv = jnp.full((1, 128), 2**30, jnp.int32)
    endv = jnp.zeros((1, 128), jnp.int32)
    prev = jnp.int32(0)
    for j in range(nseq):
        startv = jnp.where(lane == 64 + j, prev, startv)
        endv = jnp.where(lane == 64 + j, ends[j], endv)
        prev = ends[j]
    lane_c = lax.broadcasted_iota(jnp.int32, (chunk, 128), 1)
    low = lane_c < 64
    segl = (lane_c >= 64) & (lane_c < 64 + nseq)
    ml = 64 + nseq
    for c in range(nch):
        lc = jnp.bitwise_xor(m, c)
        rows = slice(c * chunk, (c + 1) * chunk)
        src = qa_in if c < half else qb_in
        srows = slice(c % half * chunk, (c % half + 1) * chunk)
        rid = lc * chunk + lax.broadcasted_iota(jnp.int32, (chunk, 128), 0)
        keep = jnp.broadcast_to(mask_ref[pl.ds(lc, 1), :].astype(f32), (128, chunk)).T
        onehot = (rid >= startv) & (rid < endv)
        qfeat = jnp.where(segl, jnp.where(onehot, 1.0, 0.0), jnp.where(lane_c == ml, 1.0, 0.0))
        kfeat = jnp.where(
            segl,
            jnp.where(onehot, 0.0, -BIG),
            jnp.where(
                lane_c == ml,
                jnp.where(keep > 0.5, 0.0, -BIG),
                jnp.where((lane_c > ml) & (lane_c < ml + 4), 1.0, 0.0),
            ),
        )
        vfeat = jnp.where((lane_c >= 64) & (lane_c < 67), 1.0, 0.0)
        for h in range(heads):
            q = head_tile(src, srows, h * HD) * 0.125
            k = head_tile(src, srows, W + h * HD)
            v = head_tile(src, srows, 2 * W + h * HD)
            qa[h, rows, :] = jnp.where(low, q, qfeat).astype(bf16)
            ka[h, rows, :] = jnp.where(low, k, kfeat).astype(bf16)
            va[h, rows, :] = jnp.where(low, v, vfeat).astype(bf16)
    per, perk = chunk // BQ, chunk // BK
    lane_q = lax.broadcasted_iota(jnp.int32, (BQ, 128), 1)

    def qblock(b, _):
        off = pl.multiple_of(jnp.bitwise_xor(b // per, m) * chunk + (b % per) * BQ, BQ)
        rows = pl.ds(off, BQ)
        lo, hi = key_range(ends, b * BQ, b * BQ + BQ - 1)
        qs = [qa[h, rows, :] for h in range(heads)]
        init = []
        for h in range(heads):
            kk, vv = ka[h, rows, :].astype(f32), va[h, rows, :].astype(f32)
            own = jnp.sum(jnp.where(lane_q < 64, qs[h].astype(f32) * kk, 0.0), axis=1, keepdims=True)
            drop = jnp.sum(jnp.where(lane_q == ml, kk, 0.0), axis=1, keepdims=True) < -1.0
            init += [jnp.where(drop, own, -BIG), jnp.where(drop, vv, 0.0)]

        def kstep(kb, carry):
            koff = pl.multiple_of(jnp.bitwise_xor(kb // perk, m) * chunk + (kb % perk) * BK, BK)
            kr = pl.ds(koff, BK)
            out = []
            scores = [dot(qs[h], ka[h, kr, :], NT) for h in range(heads)]
            for h in range(heads):
                mx, acc = carry[2 * h], carry[2 * h + 1]
                new = jnp.maximum(mx, jnp.max(scores[h], axis=1, keepdims=True))
                p = jnp.exp(scores[h] - new).astype(bf16)
                out += [new, acc * jnp.exp(mx - new) + dot(p, va[h, kr, :])]
            return tuple(out)

        fin = lax.fori_loop(lo // BK, (hi + BK - 1) // BK, kstep, tuple(init))
        outs = []
        for h in range(heads):
            mx, acc = fin[2 * h], fin[2 * h + 1]
            total = acc[:, 64:65]
            outs.append(acc * (1.0 / total))
            l1, l2, l3 = split3(mx + jnp.log(total))
            feat = jnp.where(
                lane_q == ml + 1,
                -l1,
                jnp.where(lane_q == ml + 2, -l2, jnp.where(lane_q == ml + 3, -l3, qs[h].astype(f32))),
            )
            qa[h, rows, :] = feat.astype(bf16)
        full = jnp.concatenate(pack_heads(outs, lane_q < 64), axis=1)
        of_ref[rows, :] = full
        o_ref[rows, :] = full.astype(bf16)
        return 0

    lax.fori_loop(0, G // BQ, qblock, 0)


SMEM_SPEC = pl.BlockSpec(memory_space=pltpu.SMEM)
VMEM_SPEC = pl.BlockSpec(memory_space=pltpu.VMEM)


def attend_forward(m, lengths, mask, qkv_a, qkv_b, heads, chunk):
    G = 2 * qkv_a.shape[0]
    sh = jax.ShapeDtypeStruct
    return pl.pallas_call(
        functools.partial(fwd_kernel, heads=heads, chunk=chunk, BQ=256, BK=512, nseq=lengths.shape[1]),
        out_shape=(sh((G, heads * HD), bf16), sh((G, heads * HD), f32)) + (sh((heads, G, 128), bf16),) * 3,
        in_specs=[SMEM_SPEC, SMEM_SPEC, VMEM_SPEC, VMEM_SPEC, VMEM_SPEC],
        out_specs=[VMEM_SPEC] * 5,
        compiler_params=pltpu.CompilerParams(vmem_limit_bytes=VMEM_LIMIT),
        cost_estimate=pl.CostEstimate(flops=6 * 10**9, bytes_accessed=12 * 10**6, transcendentals=6 * 10**6),
        name="attend_forward",
    )(m, lengths, mask.reshape(G // chunk, chunk), qkv_a, qkv_b)


def bwd_kernel(m_ref, len_ref, qa, ka, va, of_ref, d0, d1, d2, d3, out_ref, doa, dqs, dka, dva, *, heads, chunk, BQ, BK, nseq):
    G = qa.shape[1]
    m = m_ref[0]
    ml = 64 + nseq
    ends = seq_ends(len_ref, nseq)
    lane_c = lax.broadcasted_iota(jnp.int32, (chunk, 128), 1)
    low = lane_c < 64
    for c, d in enumerate((d0, d1, d2, d3)):
        rows = slice(c * chunk, (c + 1) * chunk)
        for h in range(heads):
            do = jnp.where(low, head_tile(d, slice(None), h * HD), 0.0)
            o = head_tile(of_ref, rows, h * HD)
            row_dot = jnp.sum(jnp.where(low, do * o, 0.0), axis=1, keepdims=True)
            r1, r2, r3 = split3(row_dot)
            doa[h, rows, :] = jnp.where(
                lane_c == 64, -r1, jnp.where(lane_c == 65, -r2, jnp.where(lane_c == 66, -r3, do))
            ).astype(bf16)
            q, k, v = (ref[h, rows, :].astype(f32) for ref in (qa, ka, va))
            drop = jnp.sum(jnp.where(lane_c == ml, k, 0.0), axis=1, keepdims=True) < -1.0
            own = jnp.sum(jnp.where(low | (lane_c > ml), q * k, 0.0), axis=1, keepdims=True)
            p_own = jnp.where(drop, jnp.exp(jnp.where(drop, own, 0.0)), 0.0)
            ds_own = p_own * (jnp.sum(jnp.where(low, do * v, 0.0), axis=1, keepdims=True) - row_dot)
            dqs[h, rows, :] = ds_own * k
            dka[h, rows, :] = ds_own * q
            dva[h, rows, :] = p_own * do
    per, perk = chunk // BQ, chunk // BK

    def qblock(b, _):
        off = pl.multiple_of(jnp.bitwise_xor(b // per, m) * chunk + (b % per) * BQ, BQ)
        rows = pl.ds(off, BQ)
        lo, hi = key_range(ends, b * BQ, b * BQ + BQ - 1)

        def kstep(kb, carry):
            koff = pl.multiple_of(jnp.bitwise_xor(kb // perk, m) * chunk + (kb % perk) * BK, BK)
            kr = pl.ds(koff, BK)
            out = []
            scores = [dot(ka[h, kr, :], qa[h, rows, :], NT) for h in range(heads)]
            dps = [dot(va[h, kr, :], doa[h, rows, :], NT) for h in range(heads)]
            for h in range(heads):
                p = jnp.exp(scores[h])
                ds = (p * dps[h]).astype(bf16)
                dva[h, kr, :] += dot(p.astype(bf16), doa[h, rows, :])
                dka[h, kr, :] += dot(ds, qa[h, rows, :])
                out.append(carry[h] + dot(ds, ka[h, kr, :], TN))
            return tuple(out)

        zeros = tuple(jnp.zeros((BQ, 128), f32) for _ in range(heads))
        fin = lax.fori_loop(lo // BK, (hi + BK - 1) // BK, kstep, zeros)
        for h in range(heads):
            dqs[h, rows, :] += fin[h]
        return 0

    lax.fori_loop(0, G // BQ, qblock, 0)
    for c in range(G // chunk):
        rows = slice(c * chunk, (c + 1) * chunk)
        parts = [dqs[h, rows, :] * 0.125 for h in range(heads)]
        parts += [dka[h, rows, :] for h in range(heads)] + [dva[h, rows, :] for h in range(heads)]
        for i, tile in enumerate(pack_heads(parts, low)):
            out_ref[rows, 128 * i : 128 * i + tile.shape[1]] = tile.astype(bf16)


def attend_backward(m, lengths, qa, ka, va, of, grads, heads, chunk):
    G = qa.shape[1]
    return pl.pallas_call(
        functools.partial(bwd_kernel, heads=heads, chunk=chunk, BQ=256, BK=256, nseq=lengths.shape[1]),
        out_shape=jax.ShapeDtypeStruct((G, 3 * heads * HD), bf16),
        in_specs=[SMEM_SPEC, SMEM_SPEC] + [VMEM_SPEC] * 8,
        out_specs=VMEM_SPEC,
        scratch_shapes=[pltpu.VMEM((heads, G, 128), bf16)] + [pltpu.VMEM((heads, G, 128), f32)] * 3,
        compiler_params=pltpu.CompilerParams(vmem_limit_bytes=VMEM_LIMIT),
        cost_estimate=pl.CostEstimate(flops=15 * 10**9, bytes_accessed=12 * 10**6, transcendentals=6 * 10**6),
        name="attend_backward",
    )(m, lengths, qa, ka, va, of, *grads)


def gelu_parts(u):
    z = jnp.abs(u) * 0.7071067811865476
    t = 1.0 / (1.0 + 0.3275911 * z)
    poly = t * (0.254829592 + t * (-0.284496736 + t * (1.421413741 + t * (-1.453152027 + t * 1.061405429))))
    e = jnp.exp(-z * z)
    tail = 0.5 * poly * e
    cdf = jnp.where(u >= 0, 1.0 - tail, tail)
    return u * cdf, cdf + u * (e * 0.3989422804014327)


def ffn_in_kernel(x_ref, w_ref, b_ref, g_ref, og_ref, v_ref, a_ref, gp_ref, e_ref, st_ref):
    u = dot(x_ref[...], w_ref[...]) + b_ref[...]
    a, gp = gelu_parts(u)
    e = dot(og_ref[...], v_ref[...])
    n = a.shape[1]
    mean = jnp.sum(a, axis=1, keepdims=True) * (1.0 / n)
    cent = a - mean
    m2 = jnp.sum(cent * cent, axis=1, keepdims=True)
    eg = e * g_ref[...]
    t1 = jnp.sum(eg, axis=1, keepdims=True)
    t2 = jnp.sum(eg * cent, axis=1, keepdims=True)
    a_ref[...] = a.astype(a_ref.dtype)
    gp_ref[...] = gp.astype(gp_ref.dtype)
    e_ref[...] = e.astype(e_ref.dtype)
    lane = lax.broadcasted_iota(jnp.int32, (a.shape[0], 128), 1)
    st = jnp.where(lane == 0, mean, jnp.where(lane == 1, m2, jnp.where(lane == 2, t1, t2)))
    st_ref[...] = st.T[:8]


def ffn_in(x, w, b, g, og, v, rows=256):
    R, D = x.shape
    F = w.shape[1]
    full = lambda i: (0, 0)
    row = lambda i: (i, 0)
    sh = jax.ShapeDtypeStruct
    return pl.pallas_call(
        ffn_in_kernel,
        grid=(R // rows,),
        in_specs=[
            pl.BlockSpec((rows, D), row),
            pl.BlockSpec((D, F), full),
            pl.BlockSpec((1, F), full),
            pl.BlockSpec((1, F), full),
            pl.BlockSpec((rows, D), row),
            pl.BlockSpec((D, F), full),
        ],
        out_specs=[pl.BlockSpec((rows, F), row)] * 3 + [pl.BlockSpec((8, rows), lambda i: (0, i))],
        out_shape=[sh((R, F), f32), sh((R, F), bf16), sh((R, F), f32), sh((8, R), f32)],
        compiler_params=pltpu.CompilerParams(vmem_limit_bytes=VMEM_LIMIT),
        cost_estimate=pl.CostEstimate(flops=4 * R * D * F, bytes_accessed=16 * R * F, transcendentals=2 * R * F),
        name="ffn_in",
    )(x, w, b, g, og, v)


def ffn_back_kernel(a_ref, gp_ref, e_ref, s0, s1, s2, s3, g_ref, b_ref, w_ref, fl_ref, du_ref, dx_ref, acc_ref, *, full_width):
    stats = [s[...] for s in (s0, s1, s2, s3)]
    n = a_ref.shape[1]
    means = [s[0:1] for s in stats]
    mean = sum(means) / len(stats)
    m2 = sum(s[1:2] + n * (mu - mean) * (mu - mean) for s, mu in zip(stats, means))
    inv = lax.rsqrt(m2 / full_width + EPS)
    c1 = sum(s[2:3] for s in stats) / full_width
    c2 = inv * sum(s[3:4] + (mu - mean) * s[2:3] for s, mu in zip(stats, means)) / full_width
    sub = lax.broadcasted_iota(jnp.int32, (128, mean.shape[1]), 0)
    cols = jnp.where(sub == 0, mean, jnp.where(sub == 1, inv, jnp.where(sub == 2, c1, c2))).T
    mean, inv, c1, c2 = (cols[:, i : i + 1] for i in range(4))
    e = e_ref[...].astype(f32)
    u = (a_ref[...].astype(f32) - mean) * inv
    fl_ref[...] = (u * g_ref[...] + b_ref[...]).astype(bf16)
    du = (gp_ref[...].astype(f32) * (inv * (e * g_ref[...] - c1 - u * c2))).astype(bf16)
    du_ref[...] = du
    dx_ref[...] = dot(du, w_ref[...], NT).astype(dx_ref.dtype)

    @pl.when(pl.program_id(0) == 0)
    def _():
        acc_ref[...] = jnp.zeros_like(acc_ref)

    acc_ref[0:1, :] += jnp.sum(e * u, axis=0, keepdims=True)
    acc_ref[1:2, :] += jnp.sum(e, axis=0, keepdims=True)
    acc_ref[2:3, :] += jnp.sum(du.astype(f32), axis=0, keepdims=True)


def ffn_back(a, gp, e, stats, g, b, w, full_width, rows=256):
    R, F = a.shape
    D = w.shape[0]
    full = lambda i: (0, 0)
    row = lambda i: (i, 0)
    sh = jax.ShapeDtypeStruct
    return pl.pallas_call(
        functools.partial(ffn_back_kernel, full_width=full_width),
        grid=(R // rows,),
        in_specs=[pl.BlockSpec((rows, F), row)] * 3
        + [pl.BlockSpec((8, rows), lambda i: (0, i))] * 4
        + [pl.BlockSpec((1, F), full), pl.BlockSpec((1, F), full), pl.BlockSpec((D, F), full)],
        out_specs=[pl.BlockSpec((rows, F), row)] * 2 + [pl.BlockSpec((rows, D), row), pl.BlockSpec((8, F), full)],
        out_shape=[sh((R, F), bf16), sh((R, F), bf16), sh((R, D), bf16), sh((8, F), f32)],
        compiler_params=pltpu.CompilerParams(vmem_limit_bytes=VMEM_LIMIT),
        cost_estimate=pl.CostEstimate(flops=2 * R * D * F, bytes_accessed=16 * R * F, transcendentals=0),
        name="ffn_back",
    )(a, gp, e, *stats, g, b, w)


def norm(values, gain, bias):
    mean = jnp.mean(values, axis=-1, keepdims=True)
    cent = values - mean
    inv = lax.rsqrt(jnp.mean(cent * cent, axis=-1, keepdims=True) + EPS)
    unit = cent * inv
    return unit * gain + bias, unit, inv


def norm_back(grad, unit, inv, gain):
    scaled = grad * gain
    first = jnp.mean(scaled, axis=-1, keepdims=True)
    second = jnp.mean(scaled * unit, axis=-1, keepdims=True)
    return inv * (scaled - first - unit * second), jnp.sum(grad * unit, axis=0), jnp.sum(grad, axis=0)


def swap(x, axis, k):
    n = lax.axis_size(axis)
    return lax.ppermute(x, axis, [(i, i ^ k) for i in range(n)])


def shift(x, axis, k):
    n = lax.axis_size(axis)
    return lax.ppermute(x, axis, [(i, (i + k) % n) for i in range(n)])


def gather_rows(x):
    x2 = swap(x, "mp", 2)
    return [x, swap(x, "mp", 1), x2, swap(x2, "mp", 1)]


def gather_weight(w):
    n = lax.axis_size("dp")
    if n != 8:
        return lax.all_gather(w, "dp", axis=0, tiled=True)
    i = lax.axis_index("dp")
    pieces, here = [], w
    for hop in range(4):
        pieces.append((here, hop, 0))
        pieces.append((swap(here, "dp", 1), hop, 1))
        if hop < 3:
            here = shift(here, "dp", 2)
    full = jnp.zeros((n * w.shape[0], w.shape[1]), w.dtype)
    for piece, hop, k in pieces:
        owner = ((i - 2 * hop) % n) ^ k
        full = lax.dynamic_update_slice_in_dim(full, piece, owner * w.shape[0], 0)
    return full


def scatter_weight(g):
    n = lax.axis_size("dp")
    if n != 8:
        return lax.psum_scatter(g, "dp", scatter_dimension=0, tiled=True)
    i = lax.axis_index("dp")
    rows = g.shape[0] // n
    blocks = g.reshape(n // 2, 2, rows, g.shape[1])
    here = lax.dynamic_index_in_dim(blocks, i % 2, 1, keepdims=False)
    other = lax.dynamic_index_in_dim(blocks, 1 - i % 2, 1, keepdims=False)
    mine = here + swap(other.astype(bf16), "dp", 1).astype(f32)
    z = i // 2
    carry = lax.dynamic_index_in_dim(mine, (z + 3) % 4, 0, keepdims=False)
    for hop in range(1, 4):
        arrived = shift(carry.astype(bf16), "dp", 2).astype(f32)
        carry = arrived + lax.dynamic_index_in_dim(mine, (z + 3 - hop) % 4, 0, keepdims=False)
    return carry


def scatter_rows(far, near):
    f = far()
    r = f.shape[0] // 2
    pair = f[:r].astype(f32) + swap(f[r:].astype(bf16), "mp", 1).astype(f32)
    sent = swap(pair.astype(bf16), "mp", 2)
    n = near()
    own = n[:r].astype(f32) + swap(n[r:].astype(bf16), "mp", 1).astype(f32)
    return own + sent.astype(f32)


def per_device(
    layer_input,
    lengths,
    key_mask,
    input_gain,
    input_bias,
    qkv_weight,
    mixed_gain,
    mixed_bias,
    out_weight,
    ffn_gain,
    ffn_bias,
    fc1_weight,
    fc1_bias,
    hidden_gain,
    hidden_bias,
    fc2_weight,
    out_grad,
):
    R, D = layer_input.shape
    G = key_mask.shape[0]
    W = out_weight.shape[0]
    F = fc1_bias.shape[0]
    mp = lax.axis_size("mp")
    heads = W // HD
    m = lax.axis_index("mp").astype(jnp.int32)
    m1 = m.reshape(1)

    shard = qkv_weight.shape[0]
    qkv_out = jnp.concatenate([qkv_weight.reshape(shard, 3 * W), out_weight.T], axis=1)
    qkv_out = gather_weight(qkv_out)
    qkv_full, out_t = qkv_out[:, : 3 * W], qkv_out[:, 3 * W :]
    fc_full = lax.all_gather(jnp.concatenate([fc1_weight, fc2_weight.T], axis=1), "dp", axis=0, tiled=True)
    fc1_full, fc2_t = fc_full[:, :F], fc_full[:, F:]

    x = layer_input.astype(f32)
    normed, unit_in, inv_in = norm(x, input_gain, input_bias)
    xl = gather_rows(normed.astype(bf16))
    xl_a, xl_b = jnp.concatenate(xl[:2], axis=0), jnp.concatenate(xl[2:], axis=0)
    qkv_a = dot(xl_a, qkv_full).astype(bf16)
    qkv_b = dot(xl_b, qkv_full).astype(bf16)
    o, of, qa, ka, va = attend_forward(m1, lengths, key_mask, qkv_a, qkv_b, heads, R)
    attn = [o[:R]] + [swap(o[k * R : (k + 1) * R], "mp", k) for k in (1, 2, 3)]
    gains = jnp.stack([mixed_gain, mixed_bias])
    gains = gather_rows(gains)
    mixed_g = jnp.concatenate([v[0] for v in gains])
    mixed_b = jnp.concatenate([v[1] for v in gains])
    out_ts = gather_rows(out_t)
    outx = jnp.concatenate(out_ts, axis=1)
    ol, unit_mix, inv_mix = norm(jnp.concatenate(attn, axis=1).astype(f32), mixed_g, mixed_b)
    ol = ol.astype(bf16)
    h = x + dot(ol, outx, NT)
    hl, unit_ffn, inv_ffn = norm(h, ffn_gain, ffn_bias)
    hl = gather_rows(hl.astype(bf16))
    og = gather_rows(out_grad)
    hl_a, hl_b = jnp.concatenate(hl[:2], axis=0), jnp.concatenate(hl[2:], axis=0)
    og_a, og_b = jnp.concatenate(og[:2], axis=0), jnp.concatenate(og[2:], axis=0)
    b1, hg, hb = fc1_bias.reshape(1, F), hidden_gain.reshape(1, F), hidden_bias.reshape(1, F)
    in_a = ffn_in(hl_a, fc1_full, b1, hg, og_a, fc2_t)
    in_b = ffn_in(hl_b, fc1_full, b1, hg, og_b, fc2_t)
    st = jnp.concatenate([in_a[3], in_b[3]], axis=1)
    stats = [st]
    for k in (1, 2, 3):
        got = swap(st, "mp", k)
        stats.append(jnp.concatenate([got[:, (c ^ k) * R : ((c ^ k) + 1) * R] for c in range(mp)], axis=1))
    far_back = ffn_back(*in_b[:3], [s[:, 2 * R :] for s in stats], hg, hb, fc1_full, mp * F)
    near_back = ffn_back(*in_a[:3], [s[:, : 2 * R] for s in stats], hg, hb, fc1_full, mp * F)
    dhl = scatter_rows(lambda: far_back[2], lambda: near_back[2])
    fl_a, fl_b, du_a, du_b = near_back[0], far_back[0], near_back[1], far_back[1]
    hidden_sums = near_back[3] + far_back[3]
    fc2_t_grad = dot(og_a, fl_a, TN) + dot(og_b, fl_b, TN)
    fc1_grad = dot(hl_a, du_a, TN) + dot(hl_b, du_b, TN)
    fc_grad = jnp.concatenate([fc1_grad, fc2_t_grad], axis=1).astype(bf16)
    fc_grad = lax.psum_scatter(fc_grad, "dp", scatter_dimension=0, tiled=True).astype(f32)

    dh, ffn_gain_grad, ffn_bias_grad = norm_back(dhl, unit_ffn, inv_ffn, ffn_gain)
    dh = dh + out_grad.astype(f32)
    dhr = dh.astype(bf16)
    dol = dot(dhr, outx)
    datt, mixed_gain_grad, mixed_bias_grad = norm_back(dol, unit_mix, inv_mix, mixed_g)
    datt = datt.astype(bf16)
    pieces = [datt[:, :W]] + [swap(datt[:, k * W : (k + 1) * W], "mp", k) for k in (1, 2, 3)]
    dqkv = attend_backward(m1, lengths, qa, ka, va, of, pieces, heads, R)
    layer_output = h + scatter_rows(lambda: dot(fl_b, fc2_t, NT), lambda: dot(fl_a, fc2_t, NT))
    dqkv_a, dqkv_b = dqkv[: 2 * R], dqkv[2 * R :]
    dxl = scatter_rows(lambda: dot(dqkv_b, qkv_full, NT), lambda: dot(dqkv_a, qkv_full, NT))
    qkv_grad = dot(xl_a, dqkv_a, TN) + dot(xl_b, dqkv_b, TN)
    og_part = dot(ol, dhr, TN)
    out_grad_rows = scatter_rows(lambda: og_part[2 * W :], lambda: og_part[: 2 * W])
    both = scatter_weight(jnp.concatenate([qkv_grad, out_grad_rows.T], axis=1))
    din, input_gain_grad, input_bias_grad = norm_back(dxl, unit_in, inv_in, input_gain)
    input_grad = dh + din

    def placed(vector, k):
        width = mp * vector.shape[0]
        return lax.dynamic_update_slice_in_dim(
            jnp.zeros((width,), f32), vector, (m ^ k) * vector.shape[0], 0
        )

    def placed_xor(vector):
        return sum(placed(vector[k * W : (k + 1) * W], k) for k in range(mp))

    vectors = [
        input_gain_grad,
        input_bias_grad,
        placed_xor(mixed_gain_grad),
        placed_xor(mixed_bias_grad),
        ffn_gain_grad,
        ffn_bias_grad,
        placed(hidden_sums[2], 0),
        placed(hidden_sums[0], 0),
        placed(hidden_sums[1], 0),
    ]
    summed = lax.psum(jnp.concatenate(vectors), ("dp", "mp"))
    parts, at = [], 0
    for v in vectors:
        parts.append(summed[at : at + v.shape[0]])
        at += v.shape[0]
    return (
        layer_output.astype(bf16),
        input_grad,
        parts[0],
        parts[1],
        both[:, : 3 * W].reshape(shard, 3, W),
        parts[2],
        parts[3],
        both[:, 3 * W :].T,
        parts[4],
        parts[5],
        fc_grad[:, :F],
        parts[6],
        parts[7],
        parts[8],
        fc_grad[:, F:].T,
    )


def solution(mesh):
    return jax.shard_map(
        per_device,
        mesh=mesh,
        in_specs=(
            P(("dp", "mp"), None),
            P("dp", None),
            P("dp"),
            P(),
            P(),
            P("dp", None, "mp"),
            P("mp"),
            P("mp"),
            P("mp", "dp"),
            P(),
            P(),
            P("dp", "mp"),
            P("mp"),
            P("mp"),
            P("mp"),
            P("mp", "dp"),
            P(("dp", "mp"), None),
        ),
        out_specs=(
            P(("dp", "mp"), None),
            P(("dp", "mp"), None),
            P(),
            P(),
            P("dp", None, "mp"),
            P(),
            P(),
            P("mp", "dp"),
            P(),
            P(),
            P("dp", "mp"),
            P(),
            P(),
            P(),
            P("mp", "dp"),
        ),
        check_vma=False,
    )
```

time: 1100 us -> 452 us (0.41)
  waiting for transfers between devices: 469 us -> 121 us
  matrix products: 238 us -> 34.2 us
  blocking collectives: 174 us -> 41 us
  other arithmetic: 130 us -> 31.5 us
  Pallas kernels: 0 us -> 90.3 us
  starting transfers between devices: 0.6 us -> 40.4 us
  local copies, waits for them, and re-layouts: 48.7 us -> 73.6 us
  loops' own time: 16.8 us -> 0 us
    reduce_scatter x7 -> x0, waiting for transfers between devices: 370 us -> none  [the longest x4 199 us: reduce_rows(): lax.psum_scatter(product(jnp.int32(0), lax.axis_size('mp') * row_count),...]
    dot_general x38 -> x15, matrix products: 229 us -> 34.2 us  [dot(): return lax.dot_general(a, b, dims, preferred_element_type=f32)]
    ppermute x0 -> x47, waiting for transfers between devices: none -> 121 us  [the longest x41 90.6 us: swap(): return lax.ppermute(x, axis, [(i, i ^ k) for i in range(n)])]
    all_gather x6 -> x1, waiting for transfers between devices: 97.1 us -> 0.01 us  [per_device(): lax.all_gather(jnp.concatenate([fc1_weight, fc2_weight.T], axis=1), 'dp',...]
    pallas_call x0 -> x6, Pallas kernels: none -> 90.3 us  [the longest x1 31.4 us: attend_backward(): pl.pallas_call(functools.partial(bwd_kernel, heads=heads, chunk=chunk, BQ...]
    all_gather x2 -> x0, blocking collectives: 70.5 us -> none  [the longest x1 39.1 us: per_device(): lax.all_gather(qkv_weight, 'dp', axis=0, tiled=True)]
    psum x7 -> x1, blocking collectives: 104 us -> 41 us  [per_device(): summed = lax.psum(jnp.concatenate(vectors), ('dp', 'mp'))]
    reduce_sum x16 -> x7, other arithmetic: 62.6 us -> 10.2 us  [the longest x2 5.98 us: norm_back(): jnp.sum(grad * unit, axis=0)]
  transfers between devices with their start and end apart: 14 -> 49, of which waited for: 11 -> 18; matrix products, arithmetic and copies ran while one was open for 20% -> 24% of each run, Pallas kernels for 0% -> 12%
where the time goes in v1:
time: 452 us; the launch traced here: 448 us
  waiting for transfers between devices  121 us (27%)
  Pallas kernels  90.3 us (20%)
  local copies, waits for them, and re-layouts  73.6 us (16%)
  blocking collectives  41 us (9%)
  starting transfers between devices  40.4 us (9%)
  matrix products  34.2 us (8%)
  other arithmetic  31.5 us (7%)
  between operations  15.7 us (3%)
    ppermute x41, waiting for transfers between devices, swap(): return lax.ppermute(x, axis, [(i, i ^ k) for i in range(n)])  90.6 us
    psum x1, blocking collectives, per_device(): summed = lax.psum(jnp.concatenate(vectors), ('dp', 'mp'))  41 us
    dot_general x15, matrix products, dot(): return lax.dot_general(a, b, dims, preferred_element_type=f32)  34.2 us
    ppermute x41, starting transfers between devices, swap(): return lax.ppermute(x, axis, [(i, i ^ k) for i in range(n)])  33.6 us
    pallas_call x1, Pallas kernels, attend_backward(): pl.pallas_call(functools.partial(bwd_kernel, heads=heads, chunk=chunk, BQ...  31.4 us
    ppermute x6, waiting for transfers between devices, shift(): return lax.ppermute(x, axis, [(i, (i + k) % n) for i in range(n)])  30.6 us
    pallas_call x1, Pallas kernels, attend_forward(): pl.pallas_call(functools.partial(fwd_kernel, heads=heads, chunk=chunk, BQ...  24.1 us
    dynamic_update_slice x8, local copies, waits for them, and re-layouts, gather_weight(): full = lax.dynamic_update_slice_in_dim(full, piece, owner * w.shape[0], 0)  23 us
  transfers between devices with their start and end apart: 49, of which 18 were waited for; matrix products, arithmetic and copies ran while one was open for 24% of the time, Pallas kernels for 12%

profile of v1, /device:TPU:0, one launch (start us, length us, event | category | flops | bytes accessed | tf_op | source)
XLA Modules:
  0.0 447.9 jit_solution(6138285186762861129)
XLA Ops:
  18.2 4.0 collective-permute-done.2
  25.9 5.5 %collective-permute-done.14 = f32[2,192]{1,0:T(2,128)S(1)} collective-permute-done((f32[2,192]{1,0:T(2,128)}, f32[2,192]{1,0:T(2,128)S(1)}, u32[]{:S(2)}, u32[]{:S(2)}) %collective-permute-start.14) | collective-permute-done | bytes 1568 | tf_op jit(solution)/shard_map/ppermute | solution.py:374
  36.2 8.9 %collective-permute-done.6 = bf16[96,768]{0,1:T(8,128)(2,1)} collective-permute-done((bf16[96,768]{0,1:T(8,128)(2,1)S(1)}, bf16[96,768]{0,1:T(8,128)(2,1)}, u32[]{:S(2)}, u32[]{:S(2)}) %collective-permute-start.6) | collective-permute-done | bytes 147488 | tf_op jit(solution)/shard_map/ppermute | solution.py:379
  54.5 3.3 dynamic_update_slice.64
  59.9 3.5 dynamic_update_slice.66
  63.4 3.5 dynamic_update_slice.67
  80.5 24.1 %attend_forward.1 = (bf16[2048,192]{1,0:T(8,128)(2,1)}, f32[2048,192]{1,0:T(8,128)}, bf16[3,2048,128]{2,1,0:T(8,128)(2,1)}, bf16[3,2048,128]{2,1,0:T(8,128)(2,1)}, bf16[3,2048,128]{2,1,0:T(8,128)(2,1)}) custom-call(s32[1]{0:T(128)} %bitcast.m_ref, s32[1,8]{1,0:T(1,128)} %len_ref.3, s32[4,512]{1,0:T(4,128)} %reshape.123.mask_ref, ...), custom_call_target="tpu_custom_call" | custom-call | flops 6000000000 | bytes 12000000 | tf_op jit(solution)/shard_map/attend_forward/pallas_call | solution.py:169
  108.7 6.7 %collective-permute-done.11 = bf16[512,192]{1,0:T(8,128)(2,1)S(1)} collective-permute-done((bf16[512,192]{1,0:T(8,128)(2,1)S(1)}, bf16[512,192]{1,0:T(8,128)(2,1)S(1)}, u32[]{:S(2)}, u32[]{:S(2)}) %collective-permute-start.11) | collective-permute-done | bytes 196640 | tf_op jit(solution)/shard_map/ppermute | solution.py:374
  115.4 4.2 collective-permute-done.12
  127.5 16.5 %collective-permute-done.21 = bf16[512,768]{1,0:T(8,128)(2,1)S(1)} collective-permute-done((bf16[512,768]{1,0:T(8,128)(2,1)S(1)}, bf16[512,768]{1,0:T(8,128)(2,1)S(1)}, u32[]{:S(2)}, u32[]{:S(2)}) %collective-permute-start.21) | collective-permute-done | bytes 786464 | tf_op jit(solution)/shard_map/ppermute | solution.py:374
  150.7 3.3 fusion.69
  154.0 8.9 %ffn_in.2 = (f32[1024,768]{1,0:T(8,128)}, bf16[1024,768]{1,0:T(8,128)(2,1)}, f32[1024,768]{1,0:T(8,128)}, f32[8,1024]{1,0:T(8,128)}) custom-call(bf16[1024,768]{1,0:T(8,128)(2,1)} %pad_maximum_fusion.3.x_ref, bf16[768,768]{1,0:T(8,128)(2,1)} %get-tuple-element.136.w_ref, f32[1,768]{1,0:T(1,128)} %reshape.125.b_ref, f32[1,768]{1,0:T(1,128)} %reshape.126.g_ref, ...), custom_call_target="tpu_custom_call" | custom-call | flops 2415919104 | bytes 12582912 | tf_op jit(solution)/shard_map/ffn_in/pallas_call | solution.py:290
  164.3 8.9 %ffn_in.3 = (f32[1024,768]{1,0:T(8,128)}, bf16[1024,768]{1,0:T(8,128)(2,1)}, f32[1024,768]{1,0:T(8,128)}, f32[8,1024]{1,0:T(8,128)}) custom-call(bf16[1024,768]{1,0:T(8,128)(2,1)} %constant_dynamic-update-slice_fusion.4.x_ref, bf16[768,768]{1,0:T(8,128)(2,1)} %get-tuple-element.136.w_ref, f32[1,768]{1,0:T(1,128)} %reshape.125.b_ref, ...), custom_call_target="tpu_custom_call" | custom-call | flops 2415919104 | bytes 12582912 | tf_op jit(solution)/shard_map/ffn_in/pallas_call | solution.py:290
  182.2 8.3 %ffn_back.2 = (bf16[1024,768]{1,0:T(8,128)(2,1)}, bf16[1024,768]{1,0:T(8,128)(2,1)}, bf16[1024,768]{1,0:T(8,128)(2,1)}, f32[8,768]{1,0:T(8,128)}) custom-call(f32[1024,768]{1,0:T(8,128)} %get-tuple-element.37.a_ref, bf16[1024,768]{1,0:T(8,128)(2,1)} %get-tuple-element.38.gp_ref, f32[1024,768]{1,0:T(8,128)} %get-tuple-element.39.e_ref, ...), custom_call_target="tpu_custom_call" | custom-call | flops 1207959552 | bytes 12582912 | tf_op jit(solution)/shard_map/ffn_back/pallas_call | solution.py:343
  190.5 4.3 fusion.83
  196.1 8.7 %ffn_back.3 = (bf16[1024,768]{1,0:T(8,128)(2,1)}, bf16[1024,768]{1,0:T(8,128)(2,1)}, bf16[1024,768]{1,0:T(8,128)(2,1)}, f32[8,768]{1,0:T(8,128)}) custom-call(f32[1024,768]{1,0:T(8,128)} %get-tuple-element.43.a_ref, bf16[1024,768]{1,0:T(8,128)(2,1)} %get-tuple-element.44.gp_ref, f32[1024,768]{1,0:T(8,128)} %get-tuple-element.45.e_ref, ...), custom_call_target="tpu_custom_call" | custom-call | flops 1207959552 | bytes 12582912 | tf_op jit(solution)/shard_map/ffn_back/pallas_call | solution.py:343
  204.8 3.7 add_convert_fusion
  219.6 4.3 copy.66
  239.1 10.1 %collective-permute-done.33 = bf16[512,768]{1,0:T(8,128)(2,1)} collective-permute-done((bf16[512,768]{1,0:T(8,128)(2,1)}, bf16[512,768]{1,0:T(8,128)(2,1)}, u32[]{:S(2)}, u32[]{:S(2)}) %collective-permute-start.33) | collective-permute-done | bytes 786464 | tf_op jit(solution)/shard_map/ppermute | solution.py:374
  251.6 13.8 %collective-permute-done.30 = bf16[512,768]{1,0:T(8,128)(2,1)S(1)} collective-permute-done((bf16[512,768]{1,0:T(8,128)(2,1)S(1)}, bf16[512,768]{1,0:T(8,128)(2,1)S(1)}, u32[]{:S(2)}, u32[]{:S(2)}) %collective-permute-start.30) | collective-permute-done | bytes 786464 | tf_op jit(solution)/shard_map/ppermute | solution.py:374
  265.4 3.4 convert_add_fusion.1
  277.1 6.0 %collective-permute-done.35.d2 = bf16[512,192]{1,0:T(8,128)(2,1)S(1)} collective-permute-done((bf16[512,192]{1,0:T(8,128)(2,1)S(1)}, bf16[512,192]{1,0:T(8,128)(2,1)S(1)}, u32[]{:S(2)}, u32[]{:S(2)}) %collective-permute-start.35) | collective-permute-done | bytes 196640 | tf_op jit(solution)/shard_map/ppermute | solution.py:374
  283.0 4.8 %collective-permute-done.36.d3 = bf16[512,192]{1,0:T(8,128)(2,1)S(1)} collective-permute-done((bf16[512,192]{1,0:T(8,128)(2,1)S(1)}, bf16[512,192]{1,0:T(8,128)(2,1)S(1)}, u32[]{:S(2)}, u32[]{:S(2)}) %collective-permute-start.36) | collective-permute-done | bytes 196640 | tf_op jit(solution)/shard_map/ppermute | solution.py:374
  288.6 31.4 %attend_backward.1 = bf16[2048,576]{1,0:T(8,128)(2,1)} custom-call(s32[1]{0:T(128)} %bitcast.m_ref, s32[1,8]{1,0:T(1,128)} %len_ref.3, bf16[3,2048,128]{2,1,0:T(8,128)(2,1)} %get-tuple-element.49.qa, bf16[3,2048,128]{2,1,0:T(8,128)(2,1)} %get-tuple-element.50.ka, bf16[3,2048,128]{2,1,0:T(8,128)(2,1)} %get-tuple-element.51.va, ...), custom_call_target="tpu_custom_call" | custom-call | flops 15000000512 | bytes 12000000 | tf_op jit(solution)/shard_map/attend_backward/pallas_call | solution.py:243
  324.7 7.3 %collective-permute-done.42 = bf16[192,768]{1,0:T(8,128)(2,1)S(1)} collective-permute-done((bf16[192,768]{1,0:T(8,128)(2,1)S(1)}, bf16[192,768]{1,0:T(8,128)(2,1)S(1)}, u32[]{:S(2)}, u32[]{:S(2)}) %collective-permute-start.42) | collective-permute-done | bytes 294944 | tf_op jit(solution)/shard_map/ppermute | solution.py:374
  335.6 9.4 %collective-permute-start.43 = (bf16[4,96,768]{2,1,0:T(8,128)(2,1)S(1)}, bf16[4,96,768]{2,1,0:T(8,128)(2,1)S(1)}, u32[]{:S(2)}, u32[]{:S(2)}) collective-permute-start(bf16[4,96,768]{2,1,0:T(8,128)(2,1)S(1)} %fusion.41), channel_id=1, source_target_pairs={{0,4},{4,0},{8,12},{12,8},{16,20},{20,16},{24,28},{28,24},{1,5},{5... | collective-permute-start | bytes 1769480 | tf_op jit(solution)/shard_map/ppermute | solution.py:374
  348.6 9.7 %collective-permute-done.43 = bf16[4,96,768]{2,1,0:T(8,128)(2,1)S(1)} collective-permute-done((bf16[4,96,768]{2,1,0:T(8,128)(2,1)S(1)}, bf16[4,96,768]{2,1,0:T(8,128)(2,1)S(1)}, u32[]{:S(2)}, u32[]{:S(2)}) %collective-permute-start.43) | collective-permute-done | bytes 589856 | tf_op jit(solution)/shard_map/ppermute | solution.py:374
  364.0 5.7 %collective-permute-done.44 = bf16[96,768]{1,0:T(8,128)(2,1)S(1)} collective-permute-done((bf16[96,768]{1,0:T(8,128)(2,1)S(1)}, bf16[96,768]{1,0:T(8,128)(2,1)S(1)}, u32[]{:S(2)}, u32[]{:S(2)}) %collective-permute-start.44) | collective-permute-done | bytes 147488 | tf_op jit(solution)/shard_map/ppermute | solution.py:379
  371.6 5.2 %collective-permute-done.45 = bf16[96,768]{1,0:T(8,128)(2,1)S(1)} collective-permute-done((bf16[96,768]{1,0:T(8,128)(2,1)S(1)}, bf16[96,768]{1,0:T(8,128)(2,1)S(1)}, u32[]{:S(2)}, u32[]{:S(2)}) %collective-permute-start.45) | collective-permute-done | bytes 147488 | tf_op jit(solution)/shard_map/ppermute | solution.py:379
  377.1 6.7 %collective-permute-done.46 = bf16[96,768]{1,0:T(8,128)(2,1)S(1)} collective-permute-done((bf16[96,768]{1,0:T(8,128)(2,1)S(1)}, bf16[96,768]{1,0:T(8,128)(2,1)S(1)}, u32[]{:S(2)}, u32[]{:S(2)}) %collective-permute-start.46) | collective-permute-done | bytes 147488 | tf_op jit(solution)/shard_map/ppermute | solution.py:379
  388.7 3.6 fusion.18
  392.5 41.0 %psum.7 = f32[13824]{0:T(1024)S(1)} all-reduce(f32[13824]{0:T(1024)S(1)} %constant_dynamic-update-slice_fusion.11), channel_id=1, replica_groups=mesh['dp'=8,'mp'=4] {'dp','mp'}, use_global_device_ids=true, to_apply=%region_18.19 | all-reduce | flops 13824 | bytes 110592 | tf_op jit(solution)/shard_map/psum | solution.py:546
  (360 shorter events, 143.4 us)
Async XLA Ops:
  7.2 143.5 %all-gather.2.cloned.1.call-start = ((), (), s32[]{:S(2)}) async-start(), calls=%async_computation.1 | async-start | bytes 2654208 | tf_op jit(solution)/shard_map/all_gather | solution.py:465
  10.7 22.7 %collective-permute-start.8 = (bf16[512,768]{1,0:T(8,128)(2,1)S(1)}, bf16[512,768]{1,0:T(8,128)(2,1)}, u32[]{:S(2)}, u32[]{:S(2)}) collective-permute-start(bf16[512,768]{1,0:T(8,128)(2,1)S(1)} %fusion.13), channel_id=1, source_target_pairs={{0,2},{1,3},{2,0},{3,1},{4,6},{5,7},{6,4},{7,5},{8,10},{9,11},{10,... | collective-permute-start | bytes 2359304 | tf_op jit(solution)/shard_map/ppermute | solution.py:374
  15.6 20.1 %collective-permute-start.1 = (bf16[96,768]{0,1:T(8,128)(2,1)S(1)}, bf16[96,768]{0,1:T(8,128)(2,1)S(1)}, u32[]{:S(2)}, u32[]{:S(2)}) collective-permute-start(bf16[96,768]{0,1:T(8,128)(2,1)S(1)} %pad_maximum_fusion.11), channel_id=1, source_target_pairs={{0,4},{4,0},{8,12},{12,8},{16,20},{20,16},{24,28},{28,24},{1,5},{5... | collective-permute-start | bytes 442376 | tf_op jit(solution)/shard_map/ppermute | solution.py:374
  17.1 53.4 %collective-permute-start = (bf16[512,768]{1,0:T(8,128)(2,1)S(1)}, bf16[512,768]{1,0:T(8,128)(2,1)}, u32[]{:S(2)}, u32[]{:S(2)}) collective-permute-start(bf16[512,768]{1,0:T(8,128)(2,1)S(1)} %fusion.13), channel_id=1, source_target_pairs={{0,1},{1,0},{2,3},{3,2},{4,5},{5,4},{6,7},{7,6},{8,9},{9,8},{10,11... | collective-permute-start | bytes 2359304 | tf_op jit(solution)/shard_map/ppermute | solution.py:374
  17.7 13.7 %collective-permute-start.14 = (f32[2,192]{1,0:T(2,128)}, f32[2,192]{1,0:T(2,128)S(1)}, u32[]{:S(2)}, u32[]{:S(2)}) collective-permute-start(f32[2,192]{1,0:T(2,128)} %pad_maximum_fusion.18), channel_id=1, source_target_pairs={{0,2},{1,3},{2,0},{3,1},{4,6},{5,7},{6,4},{7,5},{8,10},{9,11},{10,... | collective-permute-start | bytes 4616 | tf_op jit(solution)/shard_map/ppermute | solution.py:374
  23.0 414.8 %reduce-scatter.4.cloned.1.call-start = ((), (), s32[]{:S(2)}) async-start(), calls=%async_computation.2 | async-start | bytes 2654208
  31.4 13.7 %collective-permute-start.6 = (bf16[96,768]{0,1:T(8,128)(2,1)S(1)}, bf16[96,768]{0,1:T(8,128)(2,1)}, u32[]{:S(2)}, u32[]{:S(2)}) collective-permute-start(bf16[96,768]{0,1:T(8,128)(2,1)S(1)} %collective-permute-done.4), channel_id=1, source_target_pairs={{0,8},{4,12},{8,16},{12,20},{16,24},{20,28},{24,0},{28,4},{1,9},{5... | collective-permute-start | bytes 442376 | tf_op jit(solution)/shard_map/ppermute | solution.py:379
  33.4 42.3 %collective-permute-start.9 = (bf16[512,768]{1,0:T(8,128)(2,1)}, bf16[512,768]{1,0:T(8,128)(2,1)}, u32[]{:S(2)}, u32[]{:S(2)}) collective-permute-start(bf16[512,768]{1,0:T(8,128)(2,1)} %collective-permute-done.8), channel_id=1, source_target_pairs={{0,1},{1,0},{2,3},{3,2},{4,5},{5,4},{6,7},{7,6},{8,9},{9,8},{10,11... | collective-permute-start | bytes 2359304 | tf_op jit(solution)/shard_map/ppermute | solution.py:374
  34.2 18.7 %collective-permute-start.3 = (bf16[96,768]{0,1:T(8,128)(2,1)S(1)}, bf16[96,768]{0,1:T(8,128)(2,1)}, u32[]{:S(2)}, u32[]{:S(2)}) collective-permute-start(bf16[96,768]{0,1:T(8,128)(2,1)S(1)} %collective-permute-done.2), channel_id=1, source_target_pairs={{0,4},{4,0},{8,12},{12,8},{16,20},{20,16},{24,28},{28,24},{1,5},{5... | collective-permute-start | bytes 442376 | tf_op jit(solution)/shard_map/ppermute | solution.py:374
  35.7 24.2 %collective-permute-start.5 = (bf16[96,768]{0,1:T(8,128)(2,1)S(1)}, bf16[96,768]{0,1:T(8,128)(2,1)}, u32[]{:S(2)}, u32[]{:S(2)}) collective-permute-start(bf16[96,768]{0,1:T(8,128)(2,1)S(1)} %collective-permute-done.4), channel_id=1, source_target_pairs={{0,4},{4,0},{8,12},{12,8},{16,20},{20,16},{24,28},{28,24},{1,5},{5... | collective-permute-start | bytes 442376 | tf_op jit(solution)/shard_map/ppermute | solution.py:374
  45.1 21.9 %collective-permute-start.7 = (bf16[96,768]{0,1:T(8,128)(2,1)}, bf16[96,768]{0,1:T(8,128)(2,1)S(1)}, u32[]{:S(2)}, u32[]{:S(2)}) collective-permute-start(bf16[96,768]{0,1:T(8,128)(2,1)} %collective-permute-done.6), channel_id=1, source_target_pairs={{0,4},{4,0},{8,12},{12,8},{16,20},{20,16},{24,28},{28,24},{1,5},{5... | collective-permute-start | bytes 442376 | tf_op jit(solution)/shard_map/ppermute | solution.py:374
  52.9 72.9 %collective-permute-start.23 = (bf16[512,768]{1,0:T(8,128)(2,1)}, bf16[512,768]{1,0:T(8,128)(2,1)}, u32[]{:S(2)}, u32[]{:S(2)}) collective-permute-start(bf16[512,768]{1,0:T(8,128)(2,1)} %param.33), channel_id=1, source_target_pairs={{0,2},{1,3},{2,0},{3,1},{4,6},{5,7},{6,4},{7,5},{8,10},{9,11},{10,... | collective-permute-start | bytes 2359304 | tf_op jit(solution)/shard_map/ppermute | solution.py:374
  59.8 47.9 %collective-permute-start.15 = (f32[2,192]{1,0:T(2,128)S(1)}, f32[2,192]{1,0:T(2,128)S(1)}, u32[]{:S(2)}, u32[]{:S(2)}) collective-permute-start(f32[2,192]{1,0:T(2,128)S(1)} %collective-permute-done.14), channel_id=1, source_target_pairs={{0,1},{1,0},{2,3},{3,2},{4,5},{5,4},{6,7},{7,6},{8,9},{9,8},{10,11... | collective-permute-start | bytes 4616 | tf_op jit(solution)/shard_map/ppermute | solution.py:374
  69.9 38.1 %collective-permute-start.17 = (bf16[768,192]{0,1:T(8,128)(2,1)S(1)}, bf16[768,192]{0,1:T(8,128)(2,1)}, u32[]{:S(2)}, u32[]{:S(2)}) collective-permute-start(bf16[768,192]{0,1:T(8,128)(2,1)S(1)} %slice.313), channel_id=1, source_target_pairs={{0,2},{1,3},{2,0},{3,1},{4,6},{5,7},{6,4},{7,5},{8,10},{9,11},{10,... | collective-permute-start | bytes 884744 | tf_op jit(solution)/shard_map/ppermute | solution.py:374
  108.0 12.6 %collective-permute-start.16 = (bf16[768,192]{0,1:T(8,128)(2,1)S(1)}, bf16[768,192]{0,1:T(8,128)(2,1)S(1)}, u32[]{:S(2)}, u32[]{:S(2)}) collective-permute-start(bf16[768,192]{0,1:T(8,128)(2,1)S(1)} %slice.313), channel_id=1, source_target_pairs={{0,1},{1,0},{2,3},{3,2},{4,5},{5,4},{6,7},{7,6},{8,9},{9,8},{10,11... | collective-permute-start | bytes 884744 | tf_op jit(solution)/shard_map/ppermute | solution.py:374
  123.9 20.1 %collective-permute-start.21 = (bf16[512,768]{1,0:T(8,128)(2,1)S(1)}, bf16[512,768]{1,0:T(8,128)(2,1)S(1)}, u32[]{:S(2)}, u32[]{:S(2)}) collective-permute-start(bf16[512,768]{1,0:T(8,128)(2,1)S(1)} %add_convert_fusion.3), channel_id=1, source_target_pairs={{0,2},{1,3},{2,0},{3,1},{4,6},{5,7},{6,4},{7,5},{8,10},{9,11},{10,... | collective-permute-start | bytes 2359304 | tf_op jit(solution)/shard_map/ppermute | solution.py:374
  125.7 20.7 %collective-permute-start.20 = (bf16[512,768]{1,0:T(8,128)(2,1)}, bf16[512,768]{1,0:T(8,128)(2,1)S(1)}, u32[]{:S(2)}, u32[]{:S(2)}) collective-permute-start(bf16[512,768]{1,0:T(8,128)(2,1)} %param.33), channel_id=1, source_target_pairs={{0,1},{1,0},{2,3},{3,2},{4,5},{5,4},{6,7},{7,6},{8,9},{9,8},{10,11... | collective-permute-start | bytes 2359304 | tf_op jit(solution)/shard_map/ppermute | solution.py:374
  125.8 20.7 %collective-permute-start.24 = (bf16[512,768]{1,0:T(8,128)(2,1)}, bf16[512,768]{1,0:T(8,128)(2,1)S(1)}, u32[]{:S(2)}, u32[]{:S(2)}) collective-permute-start(bf16[512,768]{1,0:T(8,128)(2,1)} %collective-permute-done.23), channel_id=1, source_target_pairs={{0,1},{1,0},{2,3},{3,2},{4,5},{5,4},{6,7},{7,6},{8,9},{9,8},{10,11... | collective-permute-start | bytes 2359304 | tf_op jit(solution)/shard_map/ppermute | solution.py:374
  126.2 22.1 %collective-permute-start.19 = (bf16[512,768]{1,0:T(8,128)(2,1)S(1)}, bf16[512,768]{1,0:T(8,128)(2,1)S(1)}, u32[]{:S(2)}, u32[]{:S(2)}) collective-permute-start(bf16[512,768]{1,0:T(8,128)(2,1)S(1)} %add_convert_fusion.3), channel_id=1, source_target_pairs={{0,1},{1,0},{2,3},{3,2},{4,5},{5,4},{6,7},{7,6},{8,9},{9,8},{10,11... | collective-permute-start | bytes 2359304 | tf_op jit(solution)/shard_map/ppermute | solution.py:374
  211.0 24.8 %collective-permute-start.29 = (bf16[512,768]{1,0:T(8,128)(2,1)}, bf16[512,768]{1,0:T(8,128)(2,1)}, u32[]{:S(2)}, u32[]{:S(2)}) collective-permute-start(bf16[512,768]{1,0:T(8,128)(2,1)} %slice.435), channel_id=1, source_target_pairs={{0,1},{1,0},{2,3},{3,2},{4,5},{5,4},{6,7},{7,6},{8,9},{9,8},{10,11... | collective-permute-start | bytes 2359304 | tf_op jit(solution)/shard_map/ppermute | solution.py:374
  212.4 13.8 %collective-permute-start.32 = (bf16[512,768]{1,0:T(8,128)(2,1)}, bf16[512,768]{1,0:T(8,128)(2,1)}, u32[]{:S(2)}, u32[]{:S(2)}) collective-permute-start(bf16[512,768]{1,0:T(8,128)(2,1)} %slice.267), channel_id=1, source_target_pairs={{0,1},{1,0},{2,3},{3,2},{4,5},{5,4},{6,7},{7,6},{8,9},{9,8},{10,11... | collective-permute-start | bytes 2359304 | tf_op jit(solution)/shard_map/ppermute | solution.py:374
  226.1 12.9 %collective-permute-start.31 = (bf16[512,768]{1,0:T(8,128)(2,1)}, bf16[512,768]{1,0:T(8,128)(2,1)}, u32[]{:S(2)}, u32[]{:S(2)}) collective-permute-start(bf16[512,768]{1,0:T(8,128)(2,1)} %slice.265), channel_id=1, source_target_pairs={{0,1},{1,0},{2,3},{3,2},{4,5},{5,4},{6,7},{7,6},{8,9},{9,8},{10,11... | collective-permute-start | bytes 2359304 | tf_op jit(solution)/shard_map/ppermute | solution.py:374
  228.5 20.7 %collective-permute-start.33 = (bf16[512,768]{1,0:T(8,128)(2,1)}, bf16[512,768]{1,0:T(8,128)(2,1)}, u32[]{:S(2)}, u32[]{:S(2)}) collective-permute-start(bf16[512,768]{1,0:T(8,128)(2,1)} %add_convert_fusion.2), channel_id=1, source_target_pairs={{0,2},{1,3},{2,0},{3,1},{4,6},{5,7},{6,4},{7,5},{8,10},{9,11},{10,... | collective-permute-start | bytes 2359304 | tf_op jit(solution)/shard_map/ppermute | solution.py:374
  234.7 16.9 %collective-permute-start.28 = (bf16[512,768]{1,0:T(8,128)(2,1)}, bf16[512,768]{1,0:T(8,128)(2,1)}, u32[]{:S(2)}, u32[]{:S(2)}) collective-permute-start(bf16[512,768]{1,0:T(8,128)(2,1)} %slice.436), channel_id=1, source_target_pairs={{0,1},{1,0},{2,3},{3,2},{4,5},{5,4},{6,7},{7,6},{8,9},{9,8},{10,11... | collective-permute-start | bytes 2359304 | tf_op jit(solution)/shard_map/ppermute | solution.py:374
  237.6 27.7 %collective-permute-start.30 = (bf16[512,768]{1,0:T(8,128)(2,1)S(1)}, bf16[512,768]{1,0:T(8,128)(2,1)S(1)}, u32[]{:S(2)}, u32[]{:S(2)}) collective-permute-start(bf16[512,768]{1,0:T(8,128)(2,1)S(1)} %fusion.30), channel_id=1, source_target_pairs={{0,2},{1,3},{2,0},{3,1},{4,6},{5,7},{6,4},{7,5},{8,10},{9,11},{10,... | collective-permute-start | bytes 2359304 | tf_op jit(solution)/shard_map/ppermute | solution.py:374
  274.5 13.3 %collective-permute-start.36 = (bf16[512,192]{1,0:T(8,128)(2,1)S(1)}, bf16[512,192]{1,0:T(8,128)(2,1)S(1)}, u32[]{:S(2)}, u32[]{:S(2)}) collective-permute-start(bf16[512,192]{1,0:T(8,128)(2,1)S(1)} %get-tuple-element.145), channel_id=1, source_target_pairs={{0,3},{1,2},{2,1},{3,0},{4,7},{5,6},{6,5},{7,4},{8,11},{9,10},{10,... | collective-permute-start | bytes 589832 | tf_op jit(solution)/shard_map/ppermute | solution.py:374
  275.8 47.0 %collective-permute-start.41 = (bf16[192,768]{1,0:T(8,128)(2,1)S(1)}, bf16[192,768]{1,0:T(8,128)(2,1)S(1)}, u32[]{:S(2)}, u32[]{:S(2)}) collective-permute-start(bf16[192,768]{1,0:T(8,128)(2,1)S(1)} %get-tuple-element.140), channel_id=1, source_target_pairs={{0,1},{1,0},{2,3},{3,2},{4,5},{5,4},{6,7},{7,6},{8,9},{9,8},{10,11... | collective-permute-start | bytes 884744 | tf_op jit(solution)/shard_map/ppermute | solution.py:374
  276.2 48.5 %collective-permute-start.40 = (bf16[192,768]{1,0:T(8,128)(2,1)S(1)}, bf16[192,768]{1,0:T(8,128)(2,1)S(1)}, u32[]{:S(2)}, u32[]{:S(2)}) collective-permute-start(bf16[192,768]{1,0:T(8,128)(2,1)S(1)} %get-tuple-element.139), channel_id=1, source_target_pairs={{0,1},{1,0},{2,3},{3,2},{4,5},{5,4},{6,7},{7,6},{8,9},{9,8},{10,11... | collective-permute-start | bytes 884744 | tf_op jit(solution)/shard_map/ppermute | solution.py:374
  335.6 22.7 %collective-permute-start.43 = (bf16[4,96,768]{2,1,0:T(8,128)(2,1)S(1)}, bf16[4,96,768]{2,1,0:T(8,128)(2,1)S(1)}, u32[]{:S(2)}, u32[]{:S(2)}) collective-permute-start(bf16[4,96,768]{2,1,0:T(8,128)(2,1)S(1)} %fusion.41), channel_id=1, source_target_pairs={{0,4},{4,0},{8,12},{12,8},{16,20},{20,16},{24,28},{28,24},{1,5},{5... | collective-permute-start | bytes 1769480 | tf_op jit(solution)/shard_map/ppermute | solution.py:374
  348.5 21.3 %collective-permute-start.38 = (bf16[512,768]{1,0:T(8,128)(2,1)S(1)}, bf16[512,768]{1,0:T(8,128)(2,1)S(1)}, u32[]{:S(2)}, u32[]{:S(2)}) collective-permute-start(bf16[512,768]{1,0:T(8,128)(2,1)S(1)} %slice.433), channel_id=1, source_target_pairs={{0,1},{1,0},{2,3},{3,2},{4,5},{5,4},{6,7},{7,6},{8,9},{9,8},{10,11... | collective-permute-start | bytes 2359304 | tf_op jit(solution)/shard_map/ppermute | solution.py:374
  364.0 21.7 %collective-permute-start.37 = (bf16[512,768]{1,0:T(8,128)(2,1)}, bf16[512,768]{1,0:T(8,128)(2,1)S(1)}, u32[]{:S(2)}, u32[]{:S(2)}) collective-permute-start(bf16[512,768]{1,0:T(8,128)(2,1)} %slice.434), channel_id=1, source_target_pairs={{0,1},{1,0},{2,3},{3,2},{4,5},{5,4},{6,7},{7,6},{8,9},{9,8},{10,11... | collective-permute-start | bytes 2359304 | tf_op jit(solution)/shard_map/ppermute | solution.py:374
  370.9 17.8 %collective-permute-start.39 = (bf16[512,768]{1,0:T(8,128)(2,1)}, bf16[512,768]{1,0:T(8,128)(2,1)}, u32[]{:S(2)}, u32[]{:S(2)}) collective-permute-start(bf16[512,768]{1,0:T(8,128)(2,1)} %fusion.28), channel_id=1, source_target_pairs={{0,2},{1,3},{2,0},{3,1},{4,6},{5,7},{6,4},{7,5},{8,10},{9,11},{10,... | collective-permute-start | bytes 2359304 | tf_op jit(solution)/shard_map/ppermute | solution.py:374
  (86 other events, 660.2 us)
Sparse Core Ops, SparseCore 0:
  23.1 56.5 all-gather.1
  224.1 72.4 reduce-scatter.3

commit v2 on v1

v2 whole, which is shorter than its diff:
```python
import functools

import jax
import jax.numpy as jnp
from jax import lax
from jax.experimental import pallas as pl
from jax.experimental.pallas import tpu as pltpu
from jax.sharding import PartitionSpec as P

HD = 64
EPS = 1e-05
BIG = 1e30
NT = (((1,), (1,)), ((), ()))
NN = (((1,), (0,)), ((), ()))
TN = (((0,), (0,)), ((), ()))
bf16 = jnp.bfloat16
f32 = jnp.float32


def dot(a, b, dims=NN):
    return lax.dot_general(a, b, dims, preferred_element_type=f32)


def split3(x):
    high = x.astype(bf16).astype(f32)
    rest = x - high
    mid = rest.astype(bf16).astype(f32)
    return high, mid, rest - mid


def head_tile(x, col):
    at = col // 128 * 128
    tile = x[:, at : at + 128].astype(f32)
    if tile.shape[1] < 128:
        tile = jnp.concatenate([tile, jnp.zeros((tile.shape[0], 128 - tile.shape[1]), f32)], axis=1)
    return pltpu.roll(tile, 64, 1) if col % 128 else tile


def pack_heads(parts, low):
    tiles = []
    for i in range(0, len(parts), 2):
        if i + 1 < len(parts):
            tiles.append(jnp.where(low, parts[i], pltpu.roll(parts[i + 1], 64, 1)))
        else:
            tiles.append(parts[i][:, :64])
    return tiles


def seq_ends(len_ref, nseq):
    ends, total = [], jnp.int32(0)
    for j in range(nseq):
        total = total + len_ref[0, j]
        ends.append(total)
    return ends


def key_range(ends, first, last):
    lo, hi, start = jnp.int32(0), jnp.int32(0), jnp.int32(0)
    for end in ends:
        lo = jnp.where(first >= end, end, lo)
        hi = jnp.where(last >= start, end, hi)
        start = end
    return lo, hi


def prepare(m, ends, mask_ref, xs, w_ref, qas, ka, va, heads, nseq):
    chunk = xs[0].shape[0]
    W = heads * HD
    lane = lax.broadcasted_iota(jnp.int32, (1, 128), 1)
    startv = jnp.full((1, 128), 2**30, jnp.int32)
    endv = jnp.zeros((1, 128), jnp.int32)
    prev = jnp.int32(0)
    for j in range(nseq):
        startv = jnp.where(lane == 64 + j, prev, startv)
        endv = jnp.where(lane == 64 + j, ends[j], endv)
        prev = ends[j]
    lane_c = lax.broadcasted_iota(jnp.int32, (chunk, 128), 1)
    low = lane_c < 64
    segl = (lane_c >= 64) & (lane_c < 64 + nseq)
    ml = 64 + nseq
    vfeat = jnp.where((lane_c >= 64) & (lane_c < 67), 1.0, 0.0)
    for c, x_ref in enumerate(xs):
        lc = jnp.bitwise_xor(m, c)
        rows = slice(c * chunk, (c + 1) * chunk)
        qkv = dot(x_ref[...], w_ref[...]).astype(bf16)
        rid = lc * chunk + lax.broadcasted_iota(jnp.int32, (chunk, 128), 0)
        keep = jnp.broadcast_to(mask_ref[pl.ds(lc, 1), :].astype(f32), (128, chunk)).T
        onehot = (rid >= startv) & (rid < endv)
        qfeat = jnp.where(segl, jnp.where(onehot, 1.0, 0.0), jnp.where(lane_c == ml, 1.0, 0.0))
        kfeat = jnp.where(
            segl,
            jnp.where(onehot, 0.0, -BIG),
            jnp.where(
                lane_c == ml,
                jnp.where(keep > 0.5, 0.0, -BIG),
                jnp.where((lane_c > ml) & (lane_c < ml + 4), 1.0, 0.0),
            ),
        )
        for h in range(heads):
            q = head_tile(qkv, h * HD) * 0.125
            k = head_tile(qkv, W + h * HD)
            v = head_tile(qkv, 2 * W + h * HD)
            qas[c // 2][h, c % 2 * chunk : (c % 2 + 1) * chunk, :] = jnp.where(low, q, qfeat).astype(bf16)
            ka[h, rows, :] = jnp.where(low, k, kfeat).astype(bf16)
            va[h, rows, :] = jnp.where(low, v, vfeat).astype(bf16)


def attend_rows(m, ends, part, qa, qout, ka, va, outs, of_ref, *, heads, chunk, BQ, BK, nseq):
    per, perk = chunk // BQ, chunk // BK
    ml = 64 + nseq
    lane_q = lax.broadcasted_iota(jnp.int32, (BQ, 128), 1)

    def qblock(b, out_ref, c):
        first = jnp.bitwise_xor(m, c) * chunk + b * BQ
        at = pl.multiple_of(b * BQ, BQ)
        own_rows = pl.ds(pl.multiple_of(c * chunk + b * BQ, BQ), BQ)
        rows = pl.ds(pl.multiple_of(c % 2 * chunk + b * BQ, BQ), BQ)
        lo, hi = key_range(ends, first, first + BQ - 1)
        qs = [qa[h, rows, :] for h in range(heads)]
        init = []
        for h in range(heads):
            kk, vv = ka[h, own_rows, :].astype(f32), va[h, own_rows, :].astype(f32)
            own = jnp.sum(jnp.where(lane_q < 64, qs[h].astype(f32) * kk, 0.0), axis=1, keepdims=True)
            drop = jnp.sum(jnp.where(lane_q == ml, kk, 0.0), axis=1, keepdims=True) < -1.0
            init += [jnp.where(drop, own, -BIG), jnp.where(drop, vv, 0.0)]

        def kstep(kb, carry):
            koff = pl.multiple_of(jnp.bitwise_xor(kb // perk, m) * chunk + (kb % perk) * BK, BK)
            kr = pl.ds(koff, BK)
            out = []
            scores = [dot(qs[h], ka[h, kr, :], NT) for h in range(heads)]
            for h in range(heads):
                mx, acc = carry[2 * h], carry[2 * h + 1]
                new = jnp.maximum(mx, jnp.max(scores[h], axis=1, keepdims=True))
                p = jnp.exp(scores[h] - new).astype(bf16)
                out += [new, acc * jnp.exp(mx - new) + dot(p, va[h, kr, :])]
            return tuple(out)

        fin = lax.fori_loop(lo // BK, (hi + BK - 1) // BK, kstep, tuple(init))
        heads_out = []
        for h in range(heads):
            mx, acc = fin[2 * h], fin[2 * h + 1]
            total = acc[:, 64:65]
            heads_out.append(acc * (1.0 / total))
            l1, l2, l3 = split3(mx + jnp.log(total))
            feat = jnp.where(
                lane_q == ml + 1,
                -l1,
                jnp.where(lane_q == ml + 2, -l2, jnp.where(lane_q == ml + 3, -l3, qs[h].astype(f32))),
            )
            qout[h, rows, :] = feat.astype(bf16)
        full = jnp.concatenate(pack_heads(heads_out, lane_q < 64), axis=1)
        of_ref[rows, :] = full
        out_ref[pl.ds(at, BQ), :] = full.astype(bf16)

    for c, out_ref in zip((2 * part, 2 * part + 1), outs):

        def step(b, _, c=c, out_ref=out_ref):
            qblock(b, out_ref, c)
            return 0

        lax.fori_loop(0, per, step, 0)


def fwd_far_kernel(m_ref, len_ref, mask_ref, x0, x1, x2, x3, w_ref, o2, o3, of_ref, q_far, q_near, ka, va, *, heads, BQ, BK, nseq):
    m = m_ref[0]
    ends = seq_ends(len_ref, nseq)
    prepare(m, ends, mask_ref, (x0, x1, x2, x3), w_ref, (q_near, q_far), ka, va, heads, nseq)
    attend_rows(m, ends, 1, q_far, q_far, ka, va, (o2, o3), of_ref, heads=heads, chunk=x0.shape[0], BQ=BQ, BK=BK, nseq=nseq)


def fwd_near_kernel(m_ref, len_ref, q_near, ka, va, o0, o1, of_ref, q_out, *, heads, BQ, BK, nseq):
    m = m_ref[0]
    ends = seq_ends(len_ref, nseq)
    attend_rows(m, ends, 0, q_near, q_out, ka, va, (o0, o1), of_ref, heads=heads, chunk=o0.shape[0], BQ=BQ, BK=BK, nseq=nseq)


SMEM_SPEC = pl.BlockSpec(memory_space=pltpu.SMEM)
VMEM_SPEC = pl.BlockSpec(memory_space=pltpu.VMEM)
ANY_SPEC = pl.BlockSpec(memory_space=pl.ANY)
AF_VMEM = pltpu.CompilerParams(vmem_limit_bytes=24 * 2**20)
AB_VMEM = pltpu.CompilerParams(vmem_limit_bytes=42 * 2**20)
BIG_VMEM = pltpu.CompilerParams(vmem_limit_bytes=56 * 2**20)
MID_VMEM = pltpu.CompilerParams(vmem_limit_bytes=34 * 2**20)
SMALL_VMEM = pltpu.CompilerParams(vmem_limit_bytes=20 * 2**20)
sds = jax.ShapeDtypeStruct


def whole(x):
    return pl.BlockSpec(x.shape, lambda i: (0,) * x.ndim)


def tie_kernel(*refs, n, others):
    for x, out in zip(refs[:n], refs[n + others :]):
        out[...] = x[...]


def tie(xs, *others):
    n = len(xs)
    return pl.pallas_call(
        functools.partial(tie_kernel, n=n, others=len(others)),
        out_shape=[sds(x.shape, x.dtype) for x in xs],
        in_specs=[VMEM_SPEC] * n + [ANY_SPEC] * len(others),
        out_specs=[VMEM_SPEC] * n,
        compiler_params=SMALL_VMEM,
        cost_estimate=cost(1, 1),
        name="tie",
    )(*xs, *others)


def add_kernel(*refs, n):
    refs[-1][...] = sum(x[...].astype(f32) for x in refs[:n]).astype(refs[-1].dtype)


def add(xs, *others):
    return pl.pallas_call(
        functools.partial(add_kernel, n=len(xs)),
        out_shape=sds(xs[0].shape, xs[0].dtype),
        in_specs=[VMEM_SPEC] * len(xs) + [ANY_SPEC] * len(others),
        out_specs=VMEM_SPEC,
        compiler_params=SMALL_VMEM,
        cost_estimate=cost(1, 1),
        name="add",
    )(*xs, *others)


def cost(flops, nbytes, trans=0):
    return pl.CostEstimate(flops=int(flops), bytes_accessed=int(nbytes), transcendentals=int(trans))


def attend_far(m, lengths, mask, xs, w, heads):
    chunk, G = xs[0].shape[0], mask.shape[0]
    W = heads * HD
    return pl.pallas_call(
        functools.partial(fwd_far_kernel, heads=heads, BQ=256, BK=512, nseq=lengths.shape[1]),
        out_shape=(sds((chunk, W), bf16),) * 2
        + (sds((G // 2, W), f32),)
        + (sds((heads, G // 2, 128), bf16),) * 2
        + (sds((heads, G, 128), bf16),) * 2,
        in_specs=[SMEM_SPEC, SMEM_SPEC] + [VMEM_SPEC] * 6,
        out_specs=[VMEM_SPEC] * 7,
        compiler_params=AF_VMEM,
        cost_estimate=cost(20e9, 12e6, 3e6),
        name="attend_far",
    )(m, lengths, mask.reshape(G // chunk, chunk), *xs, w)


def attend_near(m, lengths, q_near, ka, va):
    heads, half, _ = q_near.shape
    W = heads * HD
    return pl.pallas_call(
        functools.partial(fwd_near_kernel, heads=heads, BQ=256, BK=512, nseq=lengths.shape[1]),
        out_shape=(sds((half // 2, W), bf16),) * 2 + (sds((half, W), f32), sds(q_near.shape, bf16)),
        in_specs=[SMEM_SPEC, SMEM_SPEC] + [VMEM_SPEC] * 3,
        out_specs=[VMEM_SPEC] * 4,
        compiler_params=AF_VMEM,
        cost_estimate=cost(20e9, 12e6, 3e6),
        name="attend_near",
    )(m, lengths, q_near, ka, va)


def bwd_kernel(m_ref, len_ref, i_ref, qn, qf, ka, va, ofn, off, d0, d1, d2, d3, x0, x1, x2, x3, w_ref, dep, out_ref, far2_ref, far_ref, here_ref, other_ref, vec_ref, qa, doa, dqs, dka, dva, grad, sums, *, heads, chunk, BQ, BK, nseq, n):
    G = ka.shape[1]
    m = m_ref[0]
    ml = 64 + nseq
    ends = seq_ends(len_ref, nseq)
    lane_c = lax.broadcasted_iota(jnp.int32, (chunk, 128), 1)
    low = lane_c < 64
    for c, d in enumerate((d0, d1, d2, d3)):
        rows = slice(c * chunk, (c + 1) * chunk)
        pair = slice(c % 2 * chunk, (c % 2 + 1) * chunk)
        for h in range(heads):
            do = jnp.where(low, head_tile(d[:chunk, :], h * HD), 0.0)
            o = head_tile((ofn, off)[c // 2][pair, :], h * HD)
            qa[h, rows, :] = (qn, qf)[c // 2][h, pair, :]
            row_dot = jnp.sum(jnp.where(low, do * o, 0.0), axis=1, keepdims=True)
            r1, r2, r3 = split3(row_dot)
            doa[h, rows, :] = jnp.where(
                lane_c == 64, -r1, jnp.where(lane_c == 65, -r2, jnp.where(lane_c == 66, -r3, do))
            ).astype(bf16)
            q, k, v = (ref[h, rows, :].astype(f32) for ref in (qa, ka, va))
            drop = jnp.sum(jnp.where(lane_c == ml, k, 0.0), axis=1, keepdims=True) < -1.0
            own = jnp.sum(jnp.where(low | (lane_c > ml), q * k, 0.0), axis=1, keepdims=True)
            p_own = jnp.where(drop, jnp.exp(jnp.where(drop, own, 0.0)), 0.0)
            ds_own = p_own * (jnp.sum(jnp.where(low, do * v, 0.0), axis=1, keepdims=True) - row_dot)
            dqs[h, rows, :] = ds_own * k
            dka[h, rows, :] = ds_own * q
            dva[h, rows, :] = p_own * do
    per, perk = chunk // BQ, chunk // BK

    def qblock(b, _):
        off = pl.multiple_of(jnp.bitwise_xor(b // per, m) * chunk + (b % per) * BQ, BQ)
        rows = pl.ds(off, BQ)
        lo, hi = key_range(ends, b * BQ, b * BQ + BQ - 1)

        def kstep(kb, carry):
            koff = pl.multiple_of(jnp.bitwise_xor(kb // perk, m) * chunk + (kb % perk) * BK, BK)
            kr = pl.ds(koff, BK)
            out = []
            scores = [dot(ka[h, kr, :], qa[h, rows, :], NT) for h in range(heads)]
            dps = [dot(va[h, kr, :], doa[h, rows, :], NT) for h in range(heads)]
            for h in range(heads):
                p = jnp.exp(scores[h])
                ds = (p * dps[h]).astype(bf16)
                dva[h, kr, :] += dot(p.astype(bf16), doa[h, rows, :])
                dka[h, kr, :] += dot(ds, qa[h, rows, :])
                out.append(carry[h] + dot(ds, ka[h, kr, :], TN))
            return tuple(out)

        zeros = tuple(jnp.zeros((BQ, 128), f32) for _ in range(heads))
        fin = lax.fori_loop(lo // BK, (hi + BK - 1) // BK, kstep, zeros)
        for h in range(heads):
            dqs[h, rows, :] += fin[h]
        return 0

    lax.fori_loop(0, G // BQ, qblock, 0)
    sums[...] = jnp.zeros_like(sums)
    for c in range(G // chunk):
        rows = slice(c * chunk, (c + 1) * chunk)
        parts = [dqs[h, rows, :] * 0.125 for h in range(heads)]
        parts += [dka[h, rows, :] for h in range(heads)] + [dva[h, rows, :] for h in range(heads)]
        for i, tile in enumerate(pack_heads(parts, low)):
            tile = tile.astype(bf16)
            cols = slice(128 * i, 128 * i + tile.shape[1])
            out_ref[rows, cols] = tile
            sums[0:1, cols] += jnp.sum(tile.astype(f32), axis=0, keepdims=True)
    far_ref[...] = dot(out_ref[3 * chunk :, :], w_ref[...], NT).astype(bf16)
    far2_ref[...] = dot(out_ref[2 * chunk : 3 * chunk, :], w_ref[...], NT).astype(bf16)
    total = dot(x0[...], out_ref[:chunk, :], TN)
    for c, x in ((1, x1), (2, x2), (3, x3)):
        total = total + dot(x[...], out_ref[c * chunk : (c + 1) * chunk, :], TN)
    grad[...] = total
    wide = w_ref[...].astype(f32)
    gain = jnp.sum(wide * total, axis=1, keepdims=True)
    bias = jnp.sum(wide * sums[0:1, :], axis=1, keepdims=True)
    lane = lax.broadcasted_iota(jnp.int32, (wide.shape[0], 128), 1)
    both = jnp.where(lane == 0, gain, bias).T
    half = wide.shape[0] // 2
    vec = [both[j : j + 1, half * k : half * (k + 1)] for j in range(2) for k in range(2)]
    vec = jnp.concatenate(vec + [jnp.zeros((4, half), f32)], axis=0)
    vec_ref[...] = vec
    take_blocks(i_ref[0], grad, here_ref, other_ref, n)
    if n == 8:
        tops = top_rows(vec[0:4], wide.shape[1])
        rows = wide.shape[0] // n
        for z in range(n // 2):
            other_ref[z, rows:] = tops


def attend_backward(m, lengths, i, qs, ka, va, ofs, grads, xs, w, n, dep):
    heads, G, _ = ka.shape
    chunk, D = grads[0].shape[0], w.shape[0]
    W3 = 3 * heads * HD
    shapes = tuple(block_shapes(D, W3, n, 16))
    return pl.pallas_call(
        functools.partial(bwd_kernel, heads=heads, chunk=chunk, BQ=256, BK=256, nseq=lengths.shape[1], n=n),
        out_shape=(sds((G, W3), bf16),) + (sds((chunk, D), bf16),) * 2 + shapes + (sds((8, D // 2), f32),),
        in_specs=[SMEM_SPEC] * 3 + [VMEM_SPEC] * 15 + [ANY_SPEC],
        out_specs=[VMEM_SPEC] * 6,
        scratch_shapes=[pltpu.VMEM((heads, G, 128), bf16)] * 2
        + [pltpu.VMEM((heads, G, 128), f32)] * 3
        + [pltpu.VMEM((D, W3), f32), pltpu.VMEM((8, W3), f32)],
        compiler_params=AB_VMEM,
        cost_estimate=cost(40e9, 12e6, 6e6),
        name="attend_backward",
    )(m, lengths, i, *qs, ka, va, *ofs, *grads, *xs, w, dep)


def gelu_parts(u):
    z = jnp.abs(u) * 0.7071067811865476
    t = 1.0 / (1.0 + 0.3275911 * z)
    poly = t * (0.254829592 + t * (-0.284496736 + t * (1.421413741 + t * (-1.453152027 + t * 1.061405429))))
    e = jnp.exp(-z * z)
    tail = 0.5 * poly * e
    cdf = jnp.where(u >= 0, 1.0 - tail, tail)
    return u * cdf, cdf + u * (e * 0.3989422804014327)


def pick(i, half, first, second):
    return jnp.where(i < half, first[...], second[...])


def ffn_in_kernel(x0, x1, og0, og1, w_ref, v_ref, b_ref, g_ref, *refs, half):
    a_ref, gp_ref, e_ref, st_ref = refs[-4:]
    i = pl.program_id(0)
    a, gp = gelu_parts(dot(pick(i, half, x0, x1), w_ref[...]) + row(b_ref))
    e = dot(pick(i, half, og0, og1), v_ref[...])
    n = a.shape[1]
    mean = jnp.sum(a, axis=1, keepdims=True) * (1.0 / n)
    cent = a - mean
    m2 = jnp.sum(cent * cent, axis=1, keepdims=True)
    eg = e * row(g_ref)
    t1 = jnp.sum(eg, axis=1, keepdims=True)
    t2 = jnp.sum(eg * cent, axis=1, keepdims=True)
    a_ref[...] = a
    gp_ref[...] = gp.astype(bf16)
    e_ref[...] = e
    lane = lax.broadcasted_iota(jnp.int32, (a.shape[0], 128), 1)
    st = jnp.where(lane == 0, mean, jnp.where(lane == 1, m2, jnp.where(lane == 2, t1, t2)))
    st_ref[...] = st.T[:8]


def ffn_in(xs, ogs, fc, b, g, part, stats, rows=256):
    R, D = xs[0].shape
    F = b.shape[0]
    half = R // rows
    full = lambda i: (0, 0)
    row = lambda i: (i, 0)
    lower = pl.BlockSpec((rows, D), lambda i: (jnp.minimum(i, half - 1), 0))
    upper = pl.BlockSpec((rows, D), lambda i: (jnp.maximum(i - half, 0), 0))
    extra = () if stats is None else (stats,)
    return pl.pallas_call(
        functools.partial(ffn_in_kernel, half=half),
        grid=(2 * half,),
        in_specs=[
            lower,
            upper,
            lower,
            upper,
            pl.BlockSpec((D, F), full),
            pl.BlockSpec((D, F), lambda i: (0, 1)),
            whole(b),
            whole(g),
        ]
        + [ANY_SPEC] * len(extra),
        out_specs=[pl.BlockSpec((rows, F), row)] * 3 + [pl.BlockSpec((8, rows), lambda i: (0, 2 * half * part + i))],
        out_shape=[sds((2 * R, F), f32), sds((2 * R, F), bf16), sds((2 * R, F), f32), sds((8, 4 * R), f32)],
        input_output_aliases={8: 3} if extra else {},
        compiler_params=SMALL_VMEM,
        cost_estimate=cost(8 * R * D * F, 32 * R * F, 4 * R * F),
        name="ffn_in",
    )(*xs, *ogs, fc, fc, b, g, *extra)


def back_rows(a_ref, gp_ref, e_ref, stats, g_ref, b_ref, full_width):
    stats = [s[...] for s in stats]
    n = a_ref.shape[1]
    means = [s[0:1] for s in stats]
    mean = sum(means) / len(stats)
    m2 = sum(s[1:2] + n * (mu - mean) * (mu - mean) for s, mu in zip(stats, means))
    inv = lax.rsqrt(m2 / full_width + EPS)
    c1 = sum(s[2:3] for s in stats) / full_width
    c2 = inv * sum(s[3:4] + (mu - mean) * s[2:3] for s, mu in zip(stats, means)) / full_width
    sub = lax.broadcasted_iota(jnp.int32, (128, mean.shape[1]), 0)
    cols = jnp.where(sub == 0, mean, jnp.where(sub == 1, inv, jnp.where(sub == 2, c1, c2))).T
    mean, inv, c1, c2 = (cols[:, j : j + 1] for j in range(4))
    gain = row(g_ref)
    e = e_ref[...].astype(f32)
    u = (a_ref[...].astype(f32) - mean) * inv
    fl = (u * gain + row(b_ref)).astype(bf16)
    du = (gp_ref[...].astype(f32) * (inv * (e * gain - c1 - u * c2))).astype(bf16)
    return fl, e, u, du


def vector_sums(acc_ref, e, u, du):
    @pl.when(pl.program_id(0) == 0)
    def _():
        acc_ref[...] = jnp.zeros_like(acc_ref)

    acc_ref[0:1, :] += jnp.sum(e * u, axis=0, keepdims=True)
    acc_ref[1:2, :] += jnp.sum(e, axis=0, keepdims=True)
    acc_ref[2:3, :] += jnp.sum(du.astype(f32), axis=0, keepdims=True)


def by_half(i, half, values, firsts, seconds):
    @pl.when(i < half)
    def _():
        for v, out in zip(values, firsts):
            out[...] = v

    @pl.when(i >= half)
    def _():
        for v, out in zip(values, seconds):
            out[...] = v


def far_back_kernel(a_ref, gp_ref, e_ref, s0, s1, s2, s3, g_ref, b_ref, w_ref, fl0, fl1, du0, du1, dx0, dxa, dxb, acc_ref, *, full_width, half):
    i = pl.program_id(0)
    fl, e, u, du = back_rows(a_ref, gp_ref, e_ref, (s0, s1, s2, s3), g_ref, b_ref, full_width)
    dx = dot(du, w_ref[...], NT).astype(bf16)
    by_half(i, half, (fl, du), (fl0, du0), (fl1, du1))

    @pl.when(i < half)
    def _():
        dx0[...] = dx

    by_half(i, half + half // 2, (dx,), (dxa,), (dxb,))
    vector_sums(acc_ref, e, u, du)


def near_back_kernel(i_ref, a_ref, gp_ref, e_ref, s0, s1, s2, s3, g_ref, b_ref, w_ref, v_ref, *refs, full_width, n):
    (x0, x1, x2, x3, og0, og1, og2, og3, fl2, fl3, du2, du3, _), refs = refs[:13], refs[13:]
    dx0, dxa, dxb, acc_ref, y0, y1, y2, y3, here_ref, other_ref, token, grad = refs
    i = pl.program_id(0)
    fl, e, u, du = back_rows(a_ref, gp_ref, e_ref, (s0, s1, s2, s3), g_ref, b_ref, full_width)
    dx = dot(du, w_ref[...], NT).astype(bf16)

    @pl.when(i == 0)
    def _():
        dx0[...] = dx

    @pl.when(i == 1)
    def _():
        half = dxa.shape[0]
        dxa[...] = dx[:half]
        dxb[...] = dx[half:]

    vector_sums(acc_ref, e, u, du)
    fl_far = pick(i, 1, fl2, fl3)
    by_half(
        i,
        1,
        (dot(fl, v_ref[...], NT).astype(bf16), dot(fl_far, v_ref[...], NT).astype(bf16)),
        (y0, y2),
        (y1, y3),
    )
    F = fl.shape[1]
    first = dot(pick(i, 1, x0, x1), du, TN) + dot(pick(i, 1, x2, x3), pick(i, 1, du2, du3), TN)
    second = dot(pick(i, 1, og0, og1), fl, TN) + dot(pick(i, 1, og2, og3), fl_far, TN)

    @pl.when(i == 0)
    def _():
        grad[:, :F] = first
        grad[:, F:] = second

    @pl.when(i == 1)
    def _():
        grad[:, :F] += first
        grad[:, F:] += second
        token[...] = jnp.zeros_like(token)
        take_blocks(i_ref[0], grad, here_ref, other_ref, n)


def take_blocks(i, grad, here_ref, other_ref, n):
    if n == 8:
        me = i % 2
        rows = grad.shape[0] // n
        for z in range(n // 2):
            at = pl.multiple_of((2 * z + me) * rows, rows)
            here_ref[z] = grad[pl.ds(at, rows), :]
            at = pl.multiple_of((2 * z + 1 - me) * rows, rows)
            other_ref[z, :rows] = grad[pl.ds(at, rows), :].astype(bf16)
    else:
        here_ref[...] = grad[...]
        other_ref[...] = jnp.zeros_like(other_ref)


def block_shapes(D, cols, n, extra=0):
    if n == 8:
        return [sds((n // 2, D // n, cols), f32), sds((n // 2, D // n + extra, cols), bf16)]
    return [sds((D, cols), f32), sds((16, 128), bf16)]


def ffn_back(parts, part, stats, g, b, fc, R, full_width, rows=256):
    a, gp, e = parts
    F, D = a.shape[1], fc.shape[0]
    half = R // rows
    line = lambda i: (i, 0)
    place = lambda k: lambda i: (0, ((2 * part + i // half) ^ k) * half + i % half)
    lower = lambda i: (jnp.minimum(i, half - 1), 0)
    upper = lambda i: (jnp.maximum(i - half, 0), 0)
    pair = lambda n: [pl.BlockSpec((rows, n), lower), pl.BlockSpec((rows, n), upper)]
    dx_specs = [
        pl.BlockSpec((rows, D), lower),
        pl.BlockSpec((rows, D), lambda i: (jnp.clip(i - half, 0, half // 2 - 1), 0)),
        pl.BlockSpec((rows, D), lambda i: (jnp.maximum(i - half - half // 2, 0), 0)),
        pl.BlockSpec((8, F), lambda i: (0, 0)),
    ]
    dx_shapes = [sds((R, D), bf16)] + [sds((R // 2, D), bf16)] * 2 + [sds((8, F), f32)]
    in_specs = (
        [pl.BlockSpec((rows, F), line)] * 3
        + [pl.BlockSpec((8, rows), place(k)) for k in range(4)]
        + [whole(g), whole(b), pl.BlockSpec((D, F), lambda i: (0, 0))]
    )
    operands = (a, gp, e, *stats, g, b, fc)
    return half, pair, in_specs, operands, dx_specs, dx_shapes


def far_back(parts, stats, g, b, fc, R, full_width):
    half, pair, in_specs, operands, dx_specs, dx_shapes = ffn_back(parts, 1, stats, g, b, fc, R, full_width)
    F = parts[0].shape[1]
    return pl.pallas_call(
        functools.partial(far_back_kernel, full_width=full_width, half=half),
        grid=(2 * half,),
        in_specs=in_specs,
        out_specs=pair(F) * 2 + dx_specs,
        out_shape=[sds((R, F), bf16)] * 4 + dx_shapes,
        compiler_params=SMALL_VMEM,
        cost_estimate=cost(1, 1),
        name="far_back",
    )(*operands)


def near_back(i, parts, stats, g, b, fc, R, full_width, hl, og, fl, du, n, dep):
    _, _, in_specs, operands, _, dx_shapes = ffn_back(parts, 0, stats, g, b, fc, R, full_width, R)
    F, D = parts[0].shape[1], fc.shape[0]
    blocks = block_shapes(D, 2 * F, n)
    shapes = dx_shapes + [sds((R, D), bf16)] * 4 + blocks + [sds((8, 128), f32)]
    return pl.pallas_call(
        functools.partial(near_back_kernel, full_width=full_width, n=n),
        grid=(2,),
        in_specs=[SMEM_SPEC]
        + in_specs
        + [pl.BlockSpec((D, F), lambda i: (0, 1))]
        + [whole(x) for x in hl + og + fl + du]
        + [ANY_SPEC],
        out_specs=[whole(x) for x in shapes],
        out_shape=shapes,
        scratch_shapes=[pltpu.VMEM((D, 2 * F), f32)],
        compiler_params=MID_VMEM,
        cost_estimate=cost(1, 1),
        name="near_back",
    )(i, *operands, fc, *hl, *og, *fl, *du, dep)


def combine_kernel(z_ref, here_ref, got_ref, *refs, extra):
    z = z_ref[0] // 2
    nz, rows, cols = here_ref.shape
    own_ref = refs[-4]
    if extra:
        vec_ref, vec_out = refs[0], refs[-5]
        vectors = vec_ref[...]
        for j in range(2):
            for i in range(2):
                parts = [got_ref[0, rows + 4 * t + 2 * j + i : rows + 4 * t + 2 * j + i + 1, :extra] for t in range(3)]
                add_to = sum(p.astype(f32) for p in parts)
                vec_out[2 * j + i : 2 * j + i + 1, :] = vectors[2 * j + i : 2 * j + i + 1, :] + add_to
        vec_out[4:, :] = jnp.zeros((4, extra), f32)
        tops = top_rows(vec_out[0:4, :], cols)
    for k, out in enumerate((own_ref,) + tuple(refs[-3:])):
        at = (z + k) % nz
        block = here_ref[pl.ds(at, 1)][0] + got_ref[pl.ds(at, 1)][0][:rows].astype(f32)
        if k:
            out[:rows, :] = block.astype(bf16)
            if extra:
                out[rows:, :] = tops
        else:
            out[...] = block


def top_rows(vectors, cols):
    half = vectors.shape[1]
    tops = jnp.concatenate(list(split3(vectors)) + [jnp.zeros((4, half), f32)], axis=0)
    return jnp.concatenate([tops, jnp.zeros((16, cols - half), f32)], axis=1).astype(bf16)


def combine(i, here, got, vec=None, deps=()):
    nz, rows, cols = here.shape
    more = 0 if vec is None else 16
    return pl.pallas_call(
        functools.partial(combine_kernel, extra=0 if vec is None else vec.shape[1]),
        out_shape=([] if vec is None else [sds(vec.shape, f32)])
        + [sds((rows, cols), f32)]
        + [sds((rows + more, cols), bf16)] * 3,
        in_specs=[SMEM_SPEC] + [VMEM_SPEC] * (2 if vec is None else 3) + [ANY_SPEC] * len(deps),
        out_specs=[VMEM_SPEC] * (4 if vec is None else 5),
        compiler_params=SMALL_VMEM,
        cost_estimate=cost(8 * rows * cols, 40 * rows * cols),
        name="combine",
    )(i, here, got, *([] if vec is None else [vec]), *deps)


def gate_kernel(*refs):
    pass


def gate(xs, *others):
    n = len(xs)
    return pl.pallas_call(
        gate_kernel,
        out_shape=[sds(x.shape, x.dtype) for x in xs],
        in_specs=[ANY_SPEC] * (n + len(others)),
        out_specs=[ANY_SPEC] * n,
        input_output_aliases={i: i for i in range(n)},
        compiler_params=SMALL_VMEM,
        cost_estimate=cost(1, 1),
        name="gate",
    )(*xs, *others)


def put_kernel(t0, t1, v_ref, q1, q2, q3, out_ref, token, *, n):
    W = t0.shape[0] // 2
    both = (t0[...].astype(f32) + t1[...].astype(f32)).T
    near, far = both[:, :W], both[:, W:]
    D = near.shape[0]
    vectors = v_ref[...]
    rows = vectors.shape[0]
    for q in (q1, q2, q3):
        vectors = vectors + q[q.shape[0] - rows :, :128].astype(f32)
    token[...] = vectors
    vectors = jnp.concatenate([vectors] * n if rows * n == D else [jnp.zeros((D, 128), f32)], axis=0)
    out_ref[:, :256] = jnp.concatenate([near, vectors[:, :64]], axis=1).astype(bf16)
    out_ref[:, 256:] = jnp.concatenate([far, vectors[:, 64:]], axis=1).astype(bf16)


def put(ts, v, qs, n):
    D = ts[0].shape[1]
    return pl.pallas_call(
        functools.partial(put_kernel, n=n),
        out_shape=[sds((D, 512), bf16), sds(v.shape, f32)],
        in_specs=[VMEM_SPEC] * 6,
        out_specs=[VMEM_SPEC] * 2,
        compiler_params=SMALL_VMEM,
        cost_estimate=cost(1, 1),
        name="put",
    )(*ts, v, *qs)


def unpack_kernel(x_ref, got_ref, out_ref, *v_refs):
    W = out_ref.shape[0]
    near = x_ref[:, :256].astype(f32)
    out_ref[...] = (near + got_ref[...].astype(f32)).T[:W]
    far = x_ref[:, 256:].astype(f32)
    vectors = jnp.concatenate([near[:, W:], far[:, W:]], axis=1)
    at = 0
    for v in v_refs:
        v[...] = vectors[at : at + v.shape[0]]
        at += v.shape[0]


def unpack(rows, got, W, sizes):
    n = rows.shape[0]
    shapes = [sds((W, n), f32)] + [sds((k // 128, 128), f32) for k in sizes]
    return pl.pallas_call(
        unpack_kernel,
        out_shape=shapes,
        in_specs=[VMEM_SPEC] * 2,
        out_specs=[VMEM_SPEC] * len(shapes),
        compiler_params=SMALL_VMEM,
        cost_estimate=cost(1, 1),
        name="unpack",
    )(rows, got)


def fc_sums_kernel(own_ref, s1, s2, s3, fc1_ref, fc2_ref):
    F = fc1_ref.shape[1]
    total = own_ref[...] + s1[...].astype(f32) + s2[...].astype(f32) + s3[...].astype(f32)
    fc1_ref[...] = total[:, :F]
    fc2_ref[...] = total[:, F:]


def fc_sums(own, got):
    rows, cols = own.shape
    return pl.pallas_call(
        fc_sums_kernel,
        out_shape=[sds((rows, cols // 2), f32)] * 2,
        in_specs=[VMEM_SPEC] * 4,
        out_specs=[VMEM_SPEC] * 2,
        compiler_params=SMALL_VMEM,
        cost_estimate=cost(1, 1),
        name="fc_sums",
    )(own, *got)


def qkv_sums_kernel(own_ref, v_ref, s1, s2, s3, *refs):
    out_ref, v_out = refs[-2:]
    rows = own_ref.shape[0]
    W = out_ref.shape[2]
    half = v_ref.shape[1]
    got = s1[...].astype(f32) + s2[...].astype(f32) + s3[...].astype(f32)
    total = own_ref[...] + got[:rows]
    for c in range(3):
        out_ref[c] = total[:, c * W : (c + 1) * W]
    tops = got[rows : rows + 8, :half]
    v_out[0:4, :] = v_ref[0:4, :] + tops[0:4] + tops[4:8] + got[rows + 8 : rows + 12, :half]
    v_out[4:8, :] = jnp.zeros((4, half), f32)


def qkv_sums(own, vec, got, W, deps):
    rows = own.shape[0]
    return pl.pallas_call(
        qkv_sums_kernel,
        out_shape=[sds((3, rows, W), f32), sds(vec.shape, f32)],
        in_specs=[VMEM_SPEC] * 5 + [ANY_SPEC] * len(deps),
        out_specs=[VMEM_SPEC] * 2,
        compiler_params=SMALL_VMEM,
        cost_estimate=cost(1, 1),
        name="qkv_sums",
    )(own, vec, *got, *deps)


def finish_kernel(v0, v1, v2, v3, b_ref, g_ref, gain_ref, bias_ref):
    v = v0[...] + v1[...] + v2[...] + v3[...]
    gain = jnp.concatenate([v[0:1], v[1:2]], axis=1)
    bias = jnp.concatenate([v[2:3], v[3:4]], axis=1)
    gain = (gain - row(b_ref) * bias) / row(g_ref)
    for t in range(gain_ref.shape[0]):
        cols = slice(128 * t, 128 * (t + 1))
        bias_ref[t : t + 1, :] = bias[:, cols]
        gain_ref[t : t + 1, :] = gain[:, cols]


def finish(vs, b, g):
    D = b.shape[0]
    return pl.pallas_call(
        finish_kernel,
        out_shape=[sds((D // 128, 128), f32)] * 2,
        in_specs=[VMEM_SPEC] * 6,
        out_specs=[VMEM_SPEC] * 2,
        compiler_params=SMALL_VMEM,
        cost_estimate=cost(1, 1),
        name="finish",
    )(*vs, b, g)


def norm_parts(values):
    mean = jnp.mean(values, axis=-1, keepdims=True)
    cent = values - mean
    inv = lax.rsqrt(jnp.mean(cent * cent, axis=-1, keepdims=True) + EPS)
    return cent * inv, inv


def pieces_norm(pieces, width):
    mean = sum(jnp.sum(p, axis=1, keepdims=True) for p in pieces) * (1.0 / width)
    cents = [p - mean for p in pieces]
    var = sum(jnp.sum(c * c, axis=1, keepdims=True) for c in cents) * (1.0 / width)
    inv = lax.rsqrt(var + EPS)
    return [c * inv for c in cents], inv


def row(ref):
    return ref[...].reshape(1, ref.shape[0])


def gain_rows(ow_ref, D):
    rows = ow_ref[D : D + 16, :].astype(f32)
    return rows[0:1] + rows[1:2] + rows[2:3], rows[3:4] + rows[4:5] + rows[5:6]


def in_norm_kernel(x_ref, g_ref, b_ref, out_ref):
    unit, _ = norm_parts(x_ref[...].astype(f32))
    out_ref[...] = (unit * row(g_ref) + row(b_ref)).astype(bf16)


def mix_kernel(p0, p1, p2, p3, w0, w1, w2, w3, x_ref, g_ref, b_ref, h_ref, hl_ref):
    D = x_ref.shape[1]
    units, _ = pieces_norm([p[...].astype(f32) for p in (p0, p1, p2, p3)], D)
    h = x_ref[...].astype(f32)
    for unit, w in zip(units, (w0, w1, w2, w3)):
        gain, bias = gain_rows(w, D)
        h = h + dot((unit * gain + bias).astype(bf16), w[:D, :], NT)
    h_ref[...] = h
    unit, _ = norm_parts(h)
    hl_ref[...] = (unit * row(g_ref) + row(b_ref)).astype(bf16)


def mix(pieces, ows, x, g, b, rows=256):
    R, D = x.shape
    W = pieces[0].shape[1]
    full = lambda i: (0, 0)
    row = lambda i: (i, 0)
    return pl.pallas_call(
        mix_kernel,
        grid=(R // rows,),
        in_specs=[pl.BlockSpec((rows, W), row)] * 4
        + [pl.BlockSpec((D + 16, W), full)] * 4
        + [pl.BlockSpec((rows, D), row), whole(g), whole(b)],
        out_specs=[pl.BlockSpec((rows, D), row)] * 2,
        out_shape=[sds((R, D), f32), sds((R, D), bf16)],
        compiler_params=SMALL_VMEM,
        cost_estimate=cost(1, 1),
        name="mix",
    )(*pieces, *ows, x, g, b)


def mix_back_kernel(m_ref, da_ref, ca_ref, cb_ref, db_ref, h_ref, og_ref, p0, p1, p2, p3, w0, w1, w2, w3, g_ref, hn_ref, hf_ref, dep0, dep1, dh_ref, q0, q1, q2, q3, on_ref, of_ref, v_ref, acc, fs_ref, ms_ref, qs_ref):
    D = h_ref.shape[1]
    m = m_ref[0]
    i = pl.program_id(0)

    @pl.when(i == 0)
    def _():
        acc[...] = jnp.zeros_like(acc)
        fs_ref[...] = jnp.zeros_like(fs_ref)
        ms_ref[...] = jnp.zeros_like(ms_ref)

    beside = pick(i, pl.num_programs(0) // 2, ca_ref, cb_ref)
    dhl = da_ref[...].astype(f32) + beside.astype(f32) + db_ref[...].astype(f32)
    unit, inv = norm_parts(h_ref[...])
    scaled = dhl * row(g_ref)
    first = jnp.mean(scaled, axis=1, keepdims=True)
    second = jnp.mean(scaled * unit, axis=1, keepdims=True)
    dh = og_ref[...].astype(f32) + inv * (scaled - first - unit * second)
    dh_ref[...] = dh
    fs_ref[0:1, :] += jnp.sum(dhl * unit, axis=0, keepdims=True)
    fs_ref[1:2, :] += jnp.sum(dhl, axis=0, keepdims=True)
    dhr = dh.astype(bf16)
    units, inv = pieces_norm([p[...].astype(f32) for p in (p0, p1, p2, p3)], D)
    scaleds = []
    for k, (unit, w) in enumerate(zip(units, (w0, w1, w2, w3))):
        gain, bias = gain_rows(w, D)
        dol = dot(dhr, w[:D, :])
        acc[k] += dot((unit * gain + bias).astype(bf16), dhr, TN)
        at = jnp.bitwise_xor(m, k)
        ms_ref[pl.ds(at, 1), :] += jnp.sum(dol * unit, axis=0, keepdims=True)
        ms_ref[pl.ds(4 + at, 1), :] += jnp.sum(dol, axis=0, keepdims=True)
        scaleds.append(dol * gain)
    first = sum(jnp.sum(s, axis=1, keepdims=True) for s in scaleds) * (1.0 / D)
    second = sum(jnp.sum(s * u, axis=1, keepdims=True) for s, u in zip(scaleds, units)) * (1.0 / D)
    R = p0.shape[0]
    at = pl.ds(pl.multiple_of(i * R, R), R)
    for k, (s, u) in enumerate(zip(scaleds, units)):
        q = (inv * (s - first - u * second)).astype(bf16)
        if k:
            qs_ref[k - 1, at, :] = q
        else:
            q0[...] = q

    @pl.when(i == pl.num_programs(0) - 1)
    def _():
        W = p0.shape[1]
        for j in range(2):
            on_ref[j * W : (j + 1) * W, :] = acc[2 * j].astype(bf16)
            of_ref[j * W : (j + 1) * W, :] = acc[2 * j + 1].astype(bf16)
        hidden = hn_ref[...] + hf_ref[...]
        v_ref[...] = jnp.zeros_like(v_ref)
        tiles = D // 128
        mixed = [jnp.concatenate([ms_ref[4 * j + k : 4 * j + k + 1, :] for k in range(4)], axis=1) for j in range(2)]
        for t in range(tiles):
            cols = slice(128 * t, 128 * (t + 1))
            for j in range(3):
                v_ref[pl.ds(4 * tiles * j + tiles * m + t, 1), :] = hidden[j : j + 1, cols]
            for j in range(2):
                at = 12 * tiles + tiles * j + t
                v_ref[at : at + 1, :] = fs_ref[j : j + 1, cols]
                at += 2 * tiles
                v_ref[at : at + 1, :] = mixed[j][:, cols]
        rows = qs_ref.shape[1]
        for k, q in enumerate((q1, q2, q3)):
            q[:rows, :] = qs_ref[k]
            q[rows:, :128] = v_ref[...].astype(bf16)
            q[rows:, 128:] = jnp.zeros((q.shape[0] - rows, q.shape[1] - 128), bf16)


def mix_back(m, da, dc, db, h, og, pieces, ows, g, hidden, deps, rows=256):
    R, D = h.shape
    W = pieces[0].shape[1]
    full = lambda i: (0, 0)
    row = lambda i: (i, 0)
    wide = pl.BlockSpec((rows, D), row)
    piece = pl.BlockSpec((rows, W), row)
    halves = R // rows // 2
    extra = 16 * D // 128
    return pl.pallas_call(
        mix_back_kernel,
        grid=(R // rows,),
        in_specs=[
            SMEM_SPEC,
            wide,
            pl.BlockSpec((rows, D), lambda i: (jnp.minimum(i, halves - 1), 0)),
            pl.BlockSpec((rows, D), lambda i: (jnp.maximum(i - halves, 0), 0)),
        ]
        + [wide] * 3
        + [piece] * 4
        + [pl.BlockSpec((D + 16, W), full)] * 4
        + [whole(g), whole(hidden[0]), whole(hidden[1])]
        + [ANY_SPEC] * 2,
        out_specs=[wide, piece]
        + [pl.BlockSpec((R + extra, W), full)] * 3
        + [pl.BlockSpec((2 * W, D), full)] * 2
        + [pl.BlockSpec((extra, 128), full)],
        out_shape=[sds((R, D), f32)]
        + [sds((R, W), bf16)]
        + [sds((R + extra, W), bf16)] * 3
        + [sds((2 * W, D), bf16)] * 2
        + [sds((extra, 128), f32)],
        scratch_shapes=[
            pltpu.VMEM((4, W, D), f32),
            pltpu.VMEM((8, D), f32),
            pltpu.VMEM((8, W), f32),
            pltpu.VMEM((3, R, W), bf16),
        ],
        compiler_params=SMALL_VMEM,
        cost_estimate=cost(2e10, 1),
        name="mix_back",
    )(m, da, *dc, db, h, og, *pieces, *ows, g, *hidden, *deps)


def last_kernel(da_ref, ca_ref, cb_ref, db_ref, x_ref, dh_ref, g_ref, out_ref):
    unit, inv = norm_parts(x_ref[...].astype(f32))
    beside = pick(pl.program_id(0), pl.num_programs(0) // 2, ca_ref, cb_ref)
    scaled = (da_ref[...].astype(f32) + beside.astype(f32) + db_ref[...].astype(f32)) * row(g_ref)
    first = jnp.mean(scaled, axis=1, keepdims=True)
    second = jnp.mean(scaled * unit, axis=1, keepdims=True)
    out_ref[...] = dh_ref[...] + inv * (scaled - first - unit * second)


def rows_call(kernel, name, arrays, vectors, out_type, rows=256):
    R, D = arrays[0].shape
    n = R // rows
    wide = pl.BlockSpec((rows, D), lambda i: (i, 0))
    lower = pl.BlockSpec((rows, D), lambda i: (jnp.minimum(i, n // 2 - 1), 0))
    upper = pl.BlockSpec((rows, D), lambda i: (jnp.maximum(i - n // 2, 0), 0))
    specs, operands = [], []
    for x in arrays:
        specs += [lower, upper] if isinstance(x, list) else [wide]
        operands += x if isinstance(x, list) else [x]
    return pl.pallas_call(
        kernel,
        grid=(n,),
        in_specs=specs + [whole(v) for v in vectors],
        out_specs=wide,
        out_shape=sds((R, D), out_type),
        compiler_params=SMALL_VMEM,
        cost_estimate=cost(20 * R * D, 16 * R * D),
        name=name,
    )(*operands, *vectors)


def project_two_kernel(x_ref, w_ref, dep, out0, outa, outb, *, half):
    y = dot(x_ref[...], w_ref[...], NT).astype(bf16)
    i = pl.program_id(0)

    @pl.when(i < half // 2)
    def _():
        outa[...] = y

    @pl.when((i >= half // 2) & (i < half))
    def _():
        outb[...] = y

    @pl.when(i >= half)
    def _():
        out0[...] = y


def project_two(x, w, R, dep, rows=256):
    D = w.shape[0]
    half = R // rows
    return pl.pallas_call(
        functools.partial(project_two_kernel, half=half),
        grid=(2 * half,),
        in_specs=[pl.BlockSpec((rows, x.shape[1]), lambda i: ((i + half) % (2 * half), 0)), whole(w), ANY_SPEC],
        out_specs=[
            pl.BlockSpec((rows, D), lambda i: (jnp.maximum(i - half, 0), 0)),
            pl.BlockSpec((rows, D), lambda i: (jnp.minimum(i, half // 2 - 1), 0)),
            pl.BlockSpec((rows, D), lambda i: (jnp.clip(i - half // 2, 0, half // 2 - 1), 0)),
        ],
        out_shape=[sds((R, D), bf16)] + [sds((R // 2, D), bf16)] * 2,
        compiler_params=SMALL_VMEM,
        cost_estimate=cost(1, 1),
        name="project_two",
    )(x, w, dep)


def swap(x, axis, k):
    n = lax.axis_size(axis)
    return lax.ppermute(x, axis, [(i, i ^ k) for i in range(n)])


def shift(x, axis, k):
    n = lax.axis_size(axis)
    return lax.ppermute(x, axis, [(i, (i + k) % n) for i in range(n)])


def place_kernel(i_ref, *refs, cols, hops):
    pieces, (gains, og_ref, x2, w_ref, ow_ref, og_out, x2_out) = refs[:hops], refs[hops:]
    rows, D = pieces[0].shape[0], w_ref.shape[0]
    for j, piece in enumerate(pieces):
        owner = jnp.bitwise_xor((i_ref[0] + hops - 2 * (j // 2)) % hops, j % 2)
        at = pl.ds(pl.multiple_of(owner * rows, rows), rows)
        w_ref[at, :] = piece[:, :cols]
        ow_ref[at, :] = piece[:, cols:]
    ow_ref[D : D + 16, :] = gains[...]
    og_out[...] = og_ref[...]


def gather_first(w, gains, cols, og, x2):
    n = lax.axis_size("dp")
    if n != 8:
        full = lax.all_gather(w, "dp", axis=0, tiled=True)
        return full[:, :cols], jnp.concatenate([full[:, cols:], gains], axis=0), og, x2
    pieces, here = [], w
    for hop in range(4):
        pieces += [here, swap(here, "dp", 1)]
        if hop < 3:
            here = shift(here, "dp", 2)
    D = n * w.shape[0]
    i = lax.axis_index("dp").astype(jnp.int32).reshape(1)
    return pl.pallas_call(
        functools.partial(place_kernel, cols=cols, hops=n),
        out_shape=(
            sds((D, cols), bf16),
            sds((D + 16, w.shape[1] - cols), bf16),
            sds(og.shape, og.dtype),
            sds(x2.shape, x2.dtype),
        ),
        in_specs=[SMEM_SPEC] + [VMEM_SPEC] * (n + 2) + [ANY_SPEC],
        out_specs=[VMEM_SPEC] * 3 + [ANY_SPEC],
        input_output_aliases={n + 3: 3},
        compiler_params=SMALL_VMEM,
        cost_estimate=cost(0, 4 * D * w.shape[1]),
        name="place",
    )(i, *pieces, gains, og, x2)


def sum_all(x):
    for axis in ("mp", "dp"):
        k, n = 1, lax.axis_size(axis)
        while k < n:
            x = x + swap(x, axis, k)
            k *= 2
    return x


def per_device(
    layer_input,
    lengths,
    key_mask,
    input_gain,
    input_bias,
    qkv_weight,
    mixed_gain,
    mixed_bias,
    out_weight,
    ffn_gain,
    ffn_bias,
    fc1_weight,
    fc1_bias,
    hidden_gain,
    hidden_bias,
    fc2_weight,
    out_grad,
):
    R, D = layer_input.shape
    W = out_weight.shape[0]
    F = fc1_bias.shape[0]
    mp = lax.axis_size("mp")
    heads = W // HD
    m = lax.axis_index("mp").astype(jnp.int32)
    m1 = m.reshape(1)
    shard = qkv_weight.shape[0]
    n_dp = lax.axis_size("dp")
    dp1 = lax.axis_index("dp").astype(jnp.int32).reshape(1)

    x0 = rows_call(in_norm_kernel, "in_norm", [layer_input], [input_gain, input_bias], bf16)
    x2 = swap(x0, "mp", 2)
    x1 = swap(x0, "mp", 1)
    gains = [t.astype(bf16) for t in split3(mixed_gain) + split3(mixed_bias)]
    gains = jnp.concatenate([jnp.stack(gains), jnp.zeros((10, W), bf16)], axis=0)
    first_w = jnp.concatenate([qkv_weight.reshape(shard, 3 * W), out_weight.T], axis=1)
    qkv_full, ow, og0, x2 = gather_first(first_w, gains, 3 * W, out_grad, x2)
    fc = lax.all_gather(jnp.concatenate([fc1_weight, fc2_weight.T], axis=1), "dp", axis=0, tiled=True)
    ow2 = swap(ow, "mp", 2)
    ow1 = swap(ow, "mp", 1)
    og2 = swap(og0, "mp", 2)
    og1 = swap(og0, "mp", 1)
    xl = [x0, x1, x2, swap(x2, "mp", 1)]

    o2, o3, of_far, q_far, q_near, ka, va = attend_far(m1, lengths, key_mask, xl, qkv_full, heads)
    o0, o1, of_near, q_near = attend_near(m1, lengths, q_near, ka, va)
    pieces = [o0] + [swap(o, "mp", k) for k, o in ((1, o1), (2, o2), (3, o3))]
    ow2, og2 = tie([ow2, og2], o0, *pieces[2:])
    ows = [ow, ow1, ow2, swap(ow2, "mp", 1)]
    og = [og0, og1, og2, swap(og2, "mp", 1)]
    h, hl0 = mix(pieces, ows, layer_input, ffn_gain, ffn_bias)
    hl2 = swap(hl0, "mp", 2)
    hl1 = swap(hl0, "mp", 1)
    near = ffn_in([hl0, hl1], og[:2], fc, fc1_bias, hidden_gain, 0, None)
    hl2 = tie([hl2], near[0])[0]
    hl = [hl0, hl1, hl2, swap(hl2, "mp", 1)]
    far = ffn_in(hl[2:], og[2:], fc, fc1_bias, hidden_gain, 1, near[3])
    stats = [far[3]] + [swap(far[3], "mp", k) for k in (1, 2, 3)]
    norm_in = (stats, hidden_gain, hidden_bias, fc, R, mp * F)
    fl2, fl3, du2, du3, dx2, dx3a, dx3b, s_far = far_back(far[:3], *norm_in)
    dx3 = jnp.concatenate([swap(dx3a, "mp", 1), swap(dx3b, "mp", 1)], axis=0)
    dx2 = (dx2.astype(f32) + dx3.astype(f32)).astype(bf16)
    arrived = swap(dx2, "mp", 2)
    dx0, dx1a, dx1b, s_near, y0, y1, y2, y3, fc_here, fc_other, token = near_back(
        dp1, near[:3], *norm_in, hl, og, [fl2, fl3], [du2, du3], n_dp, dx2
    )
    beside = [swap(dx1a, "mp", 1), swap(dx1b, "mp", 1)]
    dh, q0, q1, q2, q3, t0, t1, vectors = mix_back(
        m1, dx0, beside, arrived, h, out_grad, pieces, ows, ffn_gain, [s_near, s_far], [token, token]
    )
    grads = [q0] + [swap(q, "mp", k) for k, q in ((1, q1), (2, q2), (3, q3))]
    ts = [t0, swap(t1, "mp", 1)]
    w_rows, vectors = put(ts, vectors, grads[1:], n_dp)
    w_rows = lax.psum_scatter(w_rows, "dp", scatter_dimension=0, tiled=True)
    y2 = add([y2, swap(y3, "mp", 1)], vectors)
    if n_dp == 8:
        fc_own, *sent = combine(dp1, fc_here, swap(fc_other, "dp", 1), deps=[y2])
        fc_sent = [shift(b, "dp", 2 * k) for k, b in ((1, sent[0]), (2, sent[1]), (3, sent[2]))]
    y2 = swap(y2, "mp", 2)

    dqkv, dx2, dx3, here, other, late = attend_backward(
        m1, lengths, dp1, [q_near, q_far], ka, va, [of_near, of_far], grads, xl, qkv_full, n_dp, vectors
    )
    if n_dp == 8:
        dx3, other = gate([dx3, other], y2, *fc_sent)
    dx2 = add([dx2, swap(dx3, "mp", 1)])
    arrived = swap(dx2, "mp", 2)
    dx0, dx1a, dx1b = project_two(dqkv, qkv_full, R, dx2)
    beside = [swap(dx1a, "mp", 1), swap(dx1b, "mp", 1)]
    layer_output = (h + (y0.astype(f32) + swap(y1, "mp", 1).astype(f32) + y2.astype(f32))).astype(bf16)
    if n_dp == 8:
        fc1_grad, fc2_grad = fc_sums(fc_own, fc_sent)
        late, own, *sent = combine(dp1, here, swap(other, "dp", 1), late, [fc1_grad, dx0, layer_output])
        sent = [shift(b, "dp", 2 * k) for k, b in ((1, sent[0]), (2, sent[1]), (3, sent[2]))]
    input_grad = rows_call(last_kernel, "last", [dx0, beside, arrived, layer_input, dh], [input_gain], f32)

    far_rows = swap(w_rows[:, 256:], "mp", 2)
    sizes = [mp * F] * 3 + [D] * 4
    if n_dp == 8:
        qkv_grad, late = qkv_sums(own, late, sent, W, [input_grad])
        qkv_grad = jnp.transpose(qkv_grad, (1, 0, 2))
        gain_grad, bias_grad = finish([late] + [swap(late, "mp", k) for k in (1, 2, 3)], input_bias, input_gain)
        gain_grad, bias_grad = gain_grad.reshape(D), bias_grad.reshape(D)
        out_grads, *parts = unpack(w_rows, far_rows, W, sizes)
        parts = [v.reshape(-1) for v in parts]
    else:
        qkv_grad = lax.psum_scatter(here, "dp", scatter_dimension=0, tiled=True).reshape(shard, 3, W)
        late = sum_all(late)[:4].reshape(2, D)
        bias_grad = late[1]
        gain_grad = (late[0] - input_bias * bias_grad) / input_gain
        fc_rows = lax.psum_scatter(fc_here, "dp", scatter_dimension=0, tiled=True)
        fc1_grad, fc2_grad = fc_rows[:, :F], fc_rows[:, F:]
        out_grads = (w_rows[:, :W].astype(f32) + far_rows[:, :W].astype(f32)).T
        k = 1
        while k < n_dp:
            vectors = vectors + swap(vectors, "dp", k)
            k *= 2
        flat = vectors.reshape(-1)
        parts, at = [], 0
        for size in sizes:
            parts.append(flat[at : at + size])
            at += size
    return (
        layer_output,
        input_grad,
        gain_grad,
        bias_grad,
        qkv_grad,
        parts[5],
        parts[6],
        out_grads,
        parts[3],
        parts[4],
        fc1_grad,
        parts[2],
        parts[0],
        parts[1],
        fc2_grad.T,
    )


def solution(mesh):
    return jax.shard_map(
        per_device,
        mesh=mesh,
        in_specs=(
            P(("dp", "mp"), None),
            P("dp", None),
            P("dp"),
            P(),
            P(),
            P("dp", None, "mp"),
            P("mp"),
            P("mp"),
            P("mp", "dp"),
            P(),
            P(),
            P("dp", "mp"),
            P("mp"),
            P("mp"),
            P("mp"),
            P("mp", "dp"),
            P(("dp", "mp"), None),
        ),
        out_specs=(
            P(("dp", "mp"), None),
            P(("dp", "mp"), None),
            P(),
            P(),
            P("dp", None, "mp"),
            P(),
            P(),
            P("mp", "dp"),
            P(),
            P(),
            P("dp", "mp"),
            P(),
            P(),
            P(),
            P("mp", "dp"),
        ),
        check_vma=False,
    )
```

time: 452 us -> 292 us (0.65)
  waiting for transfers between devices: 121 us -> 64.3 us
  local copies, waits for them, and re-layouts: 73.6 us -> 31.4 us
  Pallas kernels: 90.3 us -> 132 us
  blocking collectives: 41 us -> 0 us
  matrix products: 34.2 us -> 0 us
  other arithmetic: 31.5 us -> 2.71 us
    ppermute x41 -> x44, waiting for transfers between devices: 90.6 us -> 44.6 us  [swap(): return lax.ppermute(x, axis, [(i, i ^ k) for i in range(n)])]
    psum x1 -> x0, blocking collectives: 41 us -> none  [per_device(): summed = lax.psum(jnp.concatenate(vectors), ('dp', 'mp'))]
    dot_general x15 -> x0, matrix products: 34.2 us -> none  [dot(): return lax.dot_general(a, b, dims, preferred_element_type=f32)]
    pallas_call x5 -> x24, Pallas kernels: 58.9 us -> 90.4 us  [the longest x1 18 us: near_back(): pl.pallas_call(functools.partial(near_back_kernel, full_width=full_width,...]
    dynamic_update_slice x13 -> x0, local copies, waits for them, and re-layouts: 24 us -> none  [the longest x8 23 us: gather_weight(): full = lax.dynamic_update_slice_in_dim(full, piece, owner * w.shape[0], 0)]
    slice x23 -> x1, local copies, waits for them, and re-layouts: 15.1 us -> 0.8 us  [per_device(): far_rows = swap(w_rows[:, 256:], 'mp', 2)]
    ppermute x6 -> x9, waiting for transfers between devices: 30.6 us -> 18.9 us  [shift(): return lax.ppermute(x, axis, [(i, (i + k) % n) for i in range(n)])]
    reduce_sum x7 -> x0, other arithmetic: 10.2 us -> none  [the longest x2 5.98 us: norm_back(): jnp.sum(grad * unit, axis=0)]
  transfers between devices with their start and end apart: 49 -> 55, of which waited for: 18 -> 24; matrix products, arithmetic and copies ran while one was open for 24% -> 1% of each run, Pallas kernels for 12% -> 41%
where the time goes in v2:
time: 292 us; the launch traced here: 287 us
  Pallas kernels  132 us (45%)
  waiting for transfers between devices  64.3 us (22%)
  starting transfers between devices  41.5 us (14%)
  local copies, waits for them, and re-layouts  31.4 us (11%)
  between operations  15.2 us (5%)
    ppermute x44, waiting for transfers between devices, swap(): return lax.ppermute(x, axis, [(i, i ^ k) for i in range(n)])  44.6 us
    pallas_call x1, Pallas kernels, attend_backward(): pl.pallas_call(functools.partial(bwd_kernel, heads=heads, chunk=chunk, BQ...  41.4 us
    ppermute x44, starting transfers between devices, swap(): return lax.ppermute(x, axis, [(i, i ^ k) for i in range(n)])  32.1 us
    unnamed x198, local copies, waits for them, and re-layouts  30.3 us
    ppermute x9, waiting for transfers between devices, shift(): return lax.ppermute(x, axis, [(i, (i + k) % n) for i in range(n)])  18.9 us
    pallas_call x1, Pallas kernels, near_back(): pl.pallas_call(functools.partial(near_back_kernel, full_width=full_width,...  18 us
    pallas_call x1, Pallas kernels, attend_far(): pl.pallas_call(functools.partial(fwd_far_kernel, heads=heads, BQ=256, BK=...  17.2 us
    pallas_call x2, Pallas kernels, ffn_in(): pl.pallas_call(functools.partial(ffn_in_kernel, half=half), grid=(2 * hal...  14.2 us
  transfers between devices with their start and end apart: 55, of which 24 were waited for; matrix products, arithmetic and copies ran while one was open for 1% of the time, Pallas kernels for 41%

profile of v2, /device:TPU:0, one launch (start us, length us, event | category | flops | bytes accessed | tf_op | source)
XLA Modules:
  0.0 286.9 jit_solution(16294120159442912436)
XLA Ops:
  10.4 3.0 %collective-permute-start.8 = (bf16[512,768]{1,0:T(8,128)(2,1)S(1)}, bf16[512,768]{1,0:T(8,128)(2,1)}, u32[]{:S(2)}, u32[]{:S(2)}) collective-permute-start(bf16[512,768]{1,0:T(8,128)(2,1)S(1)} %in_norm.1.x0), channel_id=1, source_target_pairs={{0,2},{1,3},{2,0},{3,1},{4,6},{5,7},{6,4},{7,5},{8,10},{9,11},{10,... | collective-permute-start | bytes 2359304 | tf_op jit(solution)/shard_map/ppermute | solution.py:1048
  15.6 5.6 %collective-permute-done.2.refs_2_ = bf16[96,768]{1,0:T(8,128)(2,1)S(1)} collective-permute-done((bf16[96,768]{1,0:T(8,128)(2,1)S(1)}, bf16[96,768]{1,0:T(8,128)(2,1)S(1)}, u32[]{:S(2)}, u32[]{:S(2)}) %collective-permute-start.2) | collective-permute-done | bytes 147488 | tf_op jit(solution)/shard_map/ppermute | solution.py:1053
  22.7 5.4 %collective-permute-done.4.refs_4_ = bf16[96,768]{1,0:T(8,128)(2,1)S(1)} collective-permute-done((bf16[96,768]{1,0:T(8,128)(2,1)S(1)}, bf16[96,768]{1,0:T(8,128)(2,1)S(1)}, u32[]{:S(2)}, u32[]{:S(2)}) %collective-permute-start.4) | collective-permute-done | bytes 147488 | tf_op jit(solution)/shard_map/ppermute | solution.py:1053
  30.3 4.8 %collective-permute-done.6.refs_6_ = bf16[96,768]{1,0:T(8,128)(2,1)S(1)} collective-permute-done((bf16[96,768]{1,0:T(8,128)(2,1)S(1)}, bf16[96,768]{1,0:T(8,128)(2,1)S(1)}, u32[]{:S(2)}, u32[]{:S(2)}) %collective-permute-start.6) | collective-permute-done | bytes 147488 | tf_op jit(solution)/shard_map/ppermute | solution.py:1053
  46.9 2.1 pad_maximum_fusion
  51.2 17.2 %attend_far.1 = (bf16[512,192]{1,0:T(8,128)(2,1)S(1)}, bf16[512,192]{1,0:T(8,128)(2,1)S(1)}, f32[1024,192]{1,0:T(8,128)S(1)}, bf16[3,1024,128]{2,1,0:T(8,128)(2,...) custom-call(s32[1]{0:T(128)} %bitcast.m_ref, ...), custom_call_target="tpu_custom_call" | custom-call | flops 20000000000 | bytes 12000000 | tf_op jit(solution)/shard_map/attend_far/pallas_call | solution.py:234
  70.9 10.1 %attend_near.1 = (bf16[512,192]{1,0:T(8,128)(2,1)S(1)}, bf16[512,192]{1,0:T(8,128)(2,1)S(1)}, f32[1024,192]{1,0:T(8,128)S(1)}, bf16[3,1024,128]{2,1,0:T(8,128)(2,1)S(1)}) custom-call(s32[1]{0:T(128)} %bitcast.m_ref, s32[1,8]{1,0:T(1,128)S(1)} %copy-done.80, bf16[3,1024,128]{2,1,0:T(8,128)(2,1)S(1)} %get-tuple-element.107.q_near, ...), custom_call_target="tpu_custom_call" | custom-call | flops 20000000000 | bytes 12000000 | tf_op jit(solution)/shard_map/attend_near/pallas_call | solution.py:251
  82.0 1.7 collective-permute-done.11.refs_3_.p2
  83.8 4.0 %collective-permute-done.12.refs_4_.p3 = bf16[512,192]{1,0:T(8,128)(2,1)S(1)} collective-permute-done((bf16[512,192]{1,0:T(8,128)(2,1)S(1)}, bf16[512,192]{1,0:T(8,128)(2,1)S(1)}, u32[]{:S(2)}, u32[]{:S(2)}) %collective-permute-start.12) | collective-permute-done | bytes 196640 | tf_op jit(solution)/shard_map/ppermute | solution.py:1048
  90.8 3.0 %mix.1 = (f32[512,768]{1,0:T(8,128)S(1)}, bf16[512,768]{1,0:T(8,128)(2,1)}) custom-call(bf16[512,192]{1,0:T(8,128)(2,1)S(1)} %get-tuple-element.110.refs_2_.p0, bf16[512,192]{1,0:T(8,128)(2,1)S(1)} %collective-permute-done.10.p1, bf16[512,192]{1,0:T(8,128)(2,1)S(1)} %collective-permute-done.11.refs_3_.p2, ...), custom_call_target="tpu_custom_call" | custom-call | flops 1 | bytes 1 | tf_op jit(solution)/shard_map/mix/pallas_call | solution.py:852
  103.1 7.1 %ffn_in.2 = (f32[1024,768]{1,0:T(8,128)S(1)}, bf16[1024,768]{1,0:T(8,128)(2,1)S(1)}, f32[1024,768]{1,0:T(8,128)S(1)}, f32[8,2048]{1,0:T(8,128)S(1)}) custom-call(bf16[512,768]{1,0:T(8,128)(2,1)} %get-tuple-element.118.x0.refs_0_, bf16[512,768]{1,0:T(8,128)(2,1)S(1)} %copy-done.28, bf16[512,768]{1,0:T(8,128)(2,1)S(1)} %get-tuple-element.115.og0.refs_4_, ...), custom_call_target="tpu_custom_call" | custom-call | flops 2415919104 | bytes 12582912 | tf_op jit(solution)/shard_map/ffn_in/pallas_call | solution.py:412
  110.2 1.7 copy-done.6
  111.9 3.4 %collective-permute-done.19.refs_0_ = bf16[512,768]{1,0:T(8,128)(2,1)} collective-permute-done((bf16[512,768]{1,0:T(8,128)(2,1)}, bf16[512,768]{1,0:T(8,128)(2,1)}, u32[]{:S(2)}, u32[]{:S(2)}) %collective-permute-start.19) | collective-permute-done | bytes 786464 | tf_op jit(solution)/shard_map/ppermute | solution.py:1048
  116.7 2.3 collective-permute-done.20.x1.refs_3_
  119.0 7.1 %ffn_in.3 = (f32[1024,768]{1,0:T(8,128)S(1)}, bf16[1024,768]{1,0:T(8,128)(2,1)S(1)}, f32[1024,768]{1,0:T(8,128)S(1)}, f32[8,2048]{1,0:T(8,128)S(1)}) custom-call(bf16[512,768]{1,0:T(8,128)(2,1)S(1)} %tie.3.x0.refs_2_, bf16[512,768]{1,0:T(8,128)(2,1)S(1)} %collective-permute-done.20.x1.refs_3_, ...), custom_call_target="tpu_custom_call", output_to_operand_aliasing={{3}: (8, {})} | custom-call | flops 2415919104 | bytes 12582912 | tf_op jit(solution)/shard_map/ffn_in/pallas_call | solution.py:412
  128.0 2.2 collective-permute-done.24.s3
  130.2 1.7 collective-permute-done.23.s2
  132.0 5.5 %far_back.1 = (bf16[512,768]{1,0:T(8,128)(2,1)S(1)}, bf16[512,768]{1,0:T(8,128)(2,1)S(1)}, bf16[512,768]{1,0:T(8,128)(2,1)S(1)}, bf16[512,768]{1,0:T(8,128)(2,1)...) custom-call(f32[1024,768]{1,0:T(8,128)S(1)} %get-tuple-element.125.a, ...), custom_call_target="tpu_custom_call" | custom-call | flops 1 | bytes 1 | tf_op jit(solution)/shard_map/far_back/pallas_call | solution.py:582
  140.8 18.0 %near_back.1 = (bf16[512,768]{1,0:T(8,128)(2,1)S(1)}, bf16[256,768]{1,0:T(8,128)(2,1)S(1)}, bf16[256,768]{1,0:T(8,128)(2,1)S(1)}, f32[8,768]{1,0:T(8,128)S(1)}, ...) custom-call(s32[1]{0:T(128)} %bitcast.1.i_ref.z_ref, ...), custom_call_target="tpu_custom_call" | custom-call | flops 1 | bytes 1 | tf_op jit(solution)/shard_map/near_back/pallas_call | solution.py:599
  161.8 5.2 %mix_back.1 = (f32[512,768]{1,0:T(8,128)S(1)}, bf16[512,192]{1,0:T(8,128)(2,1)S(1)}, bf16[608,192]{1,0:T(8,128)(2,1)S(1)}, bf16[608,192]{1,0:T(8,128)(2,1)S(1)},...) custom-call(s32[1]{0:T(128)} %bitcast.m_ref, ...), custom_call_target="tpu_custom_call" | custom-call | flops 20000000000 | bytes 1 | tf_op jit(solution)/shard_map/mix_back/pallas_call | solution.py:944
  172.0 7.0 %collective-permute-done.34.q2.d2 = bf16[608,192]{1,0:T(8,128)(2,1)S(1)} collective-permute-done((bf16[608,192]{1,0:T(8,128)(2,1)S(1)}, bf16[608,192]{1,0:T(8,128)(2,1)S(1)}, u32[]{:S(2)}, u32[]{:S(2)}) %collective-permute-start.34) | collective-permute-done | bytes 233504 | tf_op jit(solution)/shard_map/ppermute | solution.py:1048
  179.0 5.0 %collective-permute-done.35.q3.d3 = bf16[608,192]{1,0:T(8,128)(2,1)S(1)} collective-permute-done((bf16[608,192]{1,0:T(8,128)(2,1)S(1)}, bf16[608,192]{1,0:T(8,128)(2,1)S(1)}, u32[]{:S(2)}, u32[]{:S(2)}) %collective-permute-start.35) | collective-permute-done | bytes 233504 | tf_op jit(solution)/shard_map/ppermute | solution.py:1048
  191.6 1.7 collective-permute-start.39
  193.4 2.1 collective-permute-start.40
  195.5 41.4 %attend_backward.1 = (bf16[2048,576]{1,0:T(8,128)(2,1)}, bf16[512,768]{1,0:T(8,128)(2,1)S(1)}, bf16[512,768]{1,0:T(8,128)(2,1)S(1)}, f32[4,96,576]{2,1,0:T(8,128...) custom-call(s32[1]{0:T(128)} %bitcast.m_ref, s32[1,8]{1,0:T(1,128)S(1)} %copy-done.80, ...), custom_call_target="tpu_custom_call" | custom-call | flops 40000000000 | bytes 12000000 | tf_op jit(solution)/shard_map/attend_backward/pallas_call | solution.py:355
  240.0 3.1 %collective-permute-start.45 = (bf16[4,112,576]{2,1,0:T(8,128)(2,1)S(1)}, bf16[4,112,576]{2,1,0:T(8,128)(2,1)S(1)}, u32[]{:S(2)}, u32[]{:S(2)}) collective-permute-start(bf16[4,112,576]{2,1,0:T(8,128)(2,1)S(1)} %get-tuple-element.172), channel_id=1, source_target_pairs={{0,4},{4,0},{8,12},{12,8},{16,20},{20,16},{24,28},{28,24},{1,5},{5... | collective-permute-start | bytes 1548296 | tf_op jit(solution)/shard_map/ppermute | solution.py:1048
  243.1 3.0 %project_two.1 = (bf16[512,768]{1,0:T(8,128)(2,1)S(1)}, bf16[256,768]{1,0:T(8,128)(2,1)S(1)}, bf16[256,768]{1,0:T(8,128)(2,1)}) custom-call(bf16[2048,576]{1,0:T(8,128)(2,1)S(1)} %copy-done.8, bf16[768,576]{1,0:T(8,128)(2,1)S(1)} %copy-done.19, bf16[512,768]{1,0:T(8,128)(2,1)S(1)} %add.26.dep), custom_call_target="tpu_custom_call" | custom-call | flops 1 | bytes 1 | tf_op jit(solution)/shard_map/project_two/pallas_call | solution.py:1030
  247.9 9.4 %collective-permute-done.45.got_ref = bf16[4,112,576]{2,1,0:T(8,128)(2,1)S(1)} collective-permute-done((bf16[4,112,576]{2,1,0:T(8,128)(2,1)S(1)}, bf16[4,112,576]{2,1,0:T(8,128)(2,1)S(1)}, u32[]{:S(2)}, u32[]{:S(2)}) %collective-permute-start.45) | collective-permute-done | bytes 516128 | tf_op jit(solution)/shard_map/ppermute | solution.py:1048
  260.3 2.3 collective-permute-start.48
  266.0 3.2 %last.1.refs_0_ = f32[512,768]{1,0:T(8,128)} custom-call(bf16[512,768]{1,0:T(8,128)(2,1)S(1)} %get-tuple-element.167.da_ref.refs_2_, bf16[256,768]{1,0:T(8,128)(2,1)S(1)} %collective-permute-done.42.ca_ref, bf16[256,768]{1,0:T(8,128)(2,1)} %collective-permute-done.43.cb_ref, bf16[512,768]{1,0:T(8,128)(2,1)S(1)} %collective-permute-done.44.db_ref, ...), custom_call_target="tpu_custom_call" | custom-call | flops 7864320 | bytes 6291456 | tf_op jit(solution)/shard_map/last/pallas_call | solution.py:998
  269.2 3.0 %collective-permute-done.47.s2 = bf16[112,576]{1,0:T(8,128)(2,1)} collective-permute-done((bf16[112,576]{1,0:T(8,128)(2,1)}, bf16[112,576]{1,0:T(8,128)(2,1)}, u32[]{:S(2)}, u32[]{:S(2)}) %collective-permute-start.47) | collective-permute-done | bytes 129056 | tf_op jit(solution)/shard_map/ppermute | solution.py:1053
  273.6 1.9 qkv_sums.1
  (320 shorter events, 77.4 us)
Async XLA Ops:
  7.2 92.0 %all-gather.2.cloned.1.call-start = ((), (), s32[]{:S(2)}) async-start(), calls=%async_computation.1 | async-start | bytes 2654208 | tf_op jit(solution)/shard_map/all_gather | solution.py:1143
  10.4 30.5 %collective-permute-start.8 = (bf16[512,768]{1,0:T(8,128)(2,1)S(1)}, bf16[512,768]{1,0:T(8,128)(2,1)}, u32[]{:S(2)}, u32[]{:S(2)}) collective-permute-start(bf16[512,768]{1,0:T(8,128)(2,1)S(1)} %in_norm.1.x0), channel_id=1, source_target_pairs={{0,2},{1,3},{2,0},{3,1},{4,6},{5,7},{6,4},{7,5},{8,10},{9,11},{10,... | collective-permute-start | bytes 2359304 | tf_op jit(solution)/shard_map/ppermute | solution.py:1048
  21.2 16.2 %collective-permute-start.1 = (bf16[96,768]{1,0:T(8,128)(2,1)S(1)}, bf16[96,768]{1,0:T(8,128)(2,1)S(1)}, u32[]{:S(2)}, u32[]{:S(2)}) collective-permute-start(bf16[96,768]{1,0:T(8,128)(2,1)S(1)} %pad_maximum_fusion.1.refs_0_), channel_id=1, source_target_pairs={{0,4},{4,0},{8,12},{12,8},{16,20},{20,16},{24,28},{28,24},{1,5},{5... | collective-permute-start | bytes 442376 | tf_op jit(solution)/shard_map/ppermute | solution.py:1048
  28.2 9.9 %collective-permute-start.3 = (bf16[96,768]{1,0:T(8,128)(2,1)S(1)}, bf16[96,768]{1,0:T(8,128)(2,1)S(1)}, u32[]{:S(2)}, u32[]{:S(2)}) collective-permute-start(bf16[96,768]{1,0:T(8,128)(2,1)S(1)} %collective-permute-done.2.refs_2_), channel_id=1, source_target_pairs={{0,4},{4,0},{8,12},{12,8},{16,20},{20,16},{24,28},{28,24},{1,5},{5... | collective-permute-start | bytes 442376 | tf_op jit(solution)/shard_map/ppermute | solution.py:1048
  38.1 13.1 %collective-permute-start = (bf16[512,768]{1,0:T(8,128)(2,1)S(1)}, bf16[512,768]{1,0:T(8,128)(2,1)}, u32[]{:S(2)}, u32[]{:S(2)}) collective-permute-start(bf16[512,768]{1,0:T(8,128)(2,1)S(1)} %in_norm.1.x0), channel_id=1, source_target_pairs={{0,1},{1,0},{2,3},{3,2},{4,5},{5,4},{6,7},{7,6},{8,9},{9,8},{10,11... | collective-permute-start | bytes 2359304 | tf_op jit(solution)/shard_map/ppermute | solution.py:1048
  49.0 213.6 %reduce-scatter.2.cloned.1.call-start = ((), (), s32[]{:S(2)}) async-start(), calls=%async_computation.2 | async-start | bytes 884736 | tf_op jit(solution)/shard_map/reduce_scatter | solution.py:1179
  49.1 32.9 %collective-permute-start.14 = (bf16[784,192]{1,0:T(8,128)(2,1)S(1)}, bf16[784,192]{1,0:T(8,128)(2,1)S(1)}, u32[]{:S(2)}, u32[]{:S(2)}) collective-permute-start(bf16[784,192]{1,0:T(8,128)(2,1)S(1)} %get-tuple-element.114.w0), channel_id=1, source_target_pairs={{0,2},{1,3},{2,0},{3,1},{4,6},{5,7},{6,4},{7,5},{8,10},{9,11},{10,... | collective-permute-start | bytes 903176 | tf_op jit(solution)/shard_map/ppermute | solution.py:1048
  49.7 39.8 %collective-permute-start.13 = (bf16[784,192]{1,0:T(8,128)(2,1)S(1)}, bf16[784,192]{1,0:T(8,128)(2,1)S(1)}, u32[]{:S(2)}, u32[]{:S(2)}) collective-permute-start(bf16[784,192]{1,0:T(8,128)(2,1)S(1)} %get-tuple-element.114.w0), channel_id=1, source_target_pairs={{0,1},{1,0},{2,3},{3,2},{4,5},{5,4},{6,7},{7,6},{8,9},{9,8},{10,11... | collective-permute-start | bytes 903176 | tf_op jit(solution)/shard_map/ppermute | solution.py:1048
  49.7 32.4 %collective-permute-start.15 = (bf16[512,768]{1,0:T(8,128)(2,1)S(1)}, bf16[512,768]{1,0:T(8,128)(2,1)S(1)}, u32[]{:S(2)}, u32[]{:S(2)}) collective-permute-start(bf16[512,768]{1,0:T(8,128)(2,1)S(1)} %get-tuple-element.115.og0.refs_4_), channel_id=1, source_target_pairs={{0,2},{1,3},{2,0},{3,1},{4,6},{5,7},{6,4},{7,5},{8,10},{9,11},{10,... | collective-permute-start | bytes 2359304 | tf_op jit(solution)/shard_map/ppermute | solution.py:1048
  69.4 14.4 %collective-permute-start.11 = (bf16[512,192]{1,0:T(8,128)(2,1)S(1)}, bf16[512,192]{1,0:T(8,128)(2,1)S(1)}, u32[]{:S(2)}, u32[]{:S(2)}) collective-permute-start(bf16[512,192]{1,0:T(8,128)(2,1)S(1)} %get-tuple-element.112), channel_id=1, source_target_pairs={{0,2},{1,3},{2,0},{3,1},{4,6},{5,7},{6,4},{7,5},{8,10},{9,11},{10,... | collective-permute-start | bytes 589832 | tf_op jit(solution)/shard_map/ppermute | solution.py:1048
  69.4 18.4 %collective-permute-start.12 = (bf16[512,192]{1,0:T(8,128)(2,1)S(1)}, bf16[512,192]{1,0:T(8,128)(2,1)S(1)}, u32[]{:S(2)}, u32[]{:S(2)}) collective-permute-start(bf16[512,192]{1,0:T(8,128)(2,1)S(1)} %get-tuple-element.113), channel_id=1, source_target_pairs={{0,3},{1,2},{2,1},{3,0},{4,7},{5,6},{6,5},{7,4},{8,11},{9,10},{10,... | collective-permute-start | bytes 589832 | tf_op jit(solution)/shard_map/ppermute | solution.py:1048
  95.4 19.9 %collective-permute-start.19 = (bf16[512,768]{1,0:T(8,128)(2,1)}, bf16[512,768]{1,0:T(8,128)(2,1)}, u32[]{:S(2)}, u32[]{:S(2)}) collective-permute-start(bf16[512,768]{1,0:T(8,128)(2,1)} %get-tuple-element.118.x0.refs_0_), channel_id=1, source_target_pairs={{0,2},{1,3},{2,0},{3,1},{4,6},{5,7},{6,4},{7,5},{8,10},{9,11},{10,... | collective-permute-start | bytes 2359304 | tf_op jit(solution)/shard_map/ppermute | solution.py:1048
  95.9 20.8 %collective-permute-start.21 = (bf16[512,768]{1,0:T(8,128)(2,1)S(1)}, bf16[512,768]{1,0:T(8,128)(2,1)}, u32[]{:S(2)}, u32[]{:S(2)}) collective-permute-start(bf16[512,768]{1,0:T(8,128)(2,1)S(1)} %get-tuple-element.122.og0.refs_6_), channel_id=1, source_target_pairs={{0,1},{1,0},{2,3},{3,2},{4,5},{5,4},{6,7},{7,6},{8,9},{9,8},{10,11... | collective-permute-start | bytes 2359304 | tf_op jit(solution)/shard_map/ppermute | solution.py:1048
  140.1 21.6 %collective-permute-start.31 = (bf16[512,768]{1,0:T(8,128)(2,1)S(1)}, bf16[512,768]{1,0:T(8,128)(2,1)S(1)}, u32[]{:S(2)}, u32[]{:S(2)}) collective-permute-start(bf16[512,768]{1,0:T(8,128)(2,1)S(1)} %add_convert_fusion.1.refs_12_), channel_id=1, source_target_pairs={{0,2},{1,3},{2,0},{3,1},{4,6},{5,7},{6,4},{7,5},{8,10},{9,11},{10,... | collective-permute-start | bytes 2359304 | tf_op jit(solution)/shard_map/ppermute | solution.py:1048
  159.4 26.3 %collective-permute-start.28 = (bf16[512,768]{1,0:T(8,128)(2,1)}, bf16[512,768]{1,0:T(8,128)(2,1)}, u32[]{:S(2)}, u32[]{:S(2)}) collective-permute-start(bf16[512,768]{1,0:T(8,128)(2,1)} %get-tuple-element.138), channel_id=1, source_target_pairs={{0,1},{1,0},{2,3},{3,2},{4,5},{5,4},{6,7},{7,6},{8,9},{9,8},{10,11... | collective-permute-start | bytes 2359304 | tf_op jit(solution)/shard_map/ppermute | solution.py:1048
  159.5 30.4 %collective-permute-start.37 = (bf16[4,96,1536]{2,1,0:T(8,128)(2,1)}, bf16[4,96,1536]{2,1,0:T(8,128)(2,1)}, u32[]{:S(2)}, u32[]{:S(2)}) collective-permute-start(bf16[4,96,1536]{2,1,0:T(8,128)(2,1)} %get-tuple-element.162), channel_id=1, source_target_pairs={{0,4},{4,0},{8,12},{12,8},{16,20},{20,16},{24,28},{28,24},{1,5},{5... | collective-permute-start | bytes 3538952 | tf_op jit(solution)/shard_map/ppermute | solution.py:1048
  168.2 15.8 %collective-permute-start.32 = (bf16[384,768]{1,0:T(8,128)(2,1)S(1)}, bf16[384,768]{1,0:T(8,128)(2,1)S(1)}, u32[]{:S(2)}, u32[]{:S(2)}) collective-permute-start(bf16[384,768]{1,0:T(8,128)(2,1)S(1)} %get-tuple-element.146), channel_id=1, source_target_pairs={{0,1},{1,0},{2,3},{3,2},{4,5},{5,4},{6,7},{7,6},{8,9},{9,8},{10,11... | collective-permute-start | bytes 1769480 | tf_op jit(solution)/shard_map/ppermute | solution.py:1048
  168.8 10.2 %collective-permute-start.34 = (bf16[608,192]{1,0:T(8,128)(2,1)S(1)}, bf16[608,192]{1,0:T(8,128)(2,1)S(1)}, u32[]{:S(2)}, u32[]{:S(2)}) collective-permute-start(bf16[608,192]{1,0:T(8,128)(2,1)S(1)} %get-tuple-element.149), channel_id=1, source_target_pairs={{0,2},{1,3},{2,0},{3,1},{4,6},{5,7},{6,4},{7,5},{8,10},{9,11},{10,... | collective-permute-start | bytes 700424 | tf_op jit(solution)/shard_map/ppermute | solution.py:1048
  170.7 13.3 %collective-permute-start.35 = (bf16[608,192]{1,0:T(8,128)(2,1)S(1)}, bf16[608,192]{1,0:T(8,128)(2,1)S(1)}, u32[]{:S(2)}, u32[]{:S(2)}) collective-permute-start(bf16[608,192]{1,0:T(8,128)(2,1)S(1)} %get-tuple-element.150), channel_id=1, source_target_pairs={{0,3},{1,2},{2,1},{3,0},{4,7},{5,6},{6,5},{7,4},{8,11},{9,10},{10,... | collective-permute-start | bytes 700424 | tf_op jit(solution)/shard_map/ppermute | solution.py:1048
  188.3 48.6 %collective-permute-start.36 = (bf16[512,768]{1,0:T(8,128)(2,1)S(1)}, bf16[512,768]{1,0:T(8,128)(2,1)S(1)}, u32[]{:S(2)}, u32[]{:S(2)}) collective-permute-start(bf16[512,768]{1,0:T(8,128)(2,1)S(1)} %add.25.refs_0_), channel_id=1, source_target_pairs={{0,2},{1,3},{2,0},{3,1},{4,6},{5,7},{6,4},{7,5},{8,10},{9,11},{10,... | collective-permute-start | bytes 2359304 | tf_op jit(solution)/shard_map/ppermute | solution.py:1048
  191.6 45.3 %collective-permute-start.38 = (bf16[96,1536]{1,0:T(8,128)(2,1)S(1)}, bf16[96,1536]{1,0:T(8,128)(2,1)S(1)}, u32[]{:S(2)}, u32[]{:S(2)}) collective-permute-start(bf16[96,1536]{1,0:T(8,128)(2,1)S(1)} %get-tuple-element.163), channel_id=1, source_target_pairs={{0,8},{4,12},{8,16},{12,20},{16,24},{20,28},{24,0},{28,4},{1,9},{5... | collective-permute-start | bytes 884744 | tf_op jit(solution)/shard_map/ppermute | solution.py:1053
  191.6 45.3 %collective-permute-start.39 = (bf16[96,1536]{1,0:T(8,128)(2,1)S(1)}, bf16[96,1536]{1,0:T(8,128)(2,1)S(1)}, u32[]{:S(2)}, u32[]{:S(2)}) collective-permute-start(bf16[96,1536]{1,0:T(8,128)(2,1)S(1)} %get-tuple-element.164), channel_id=1, source_target_pairs={{0,16},{4,20},{8,24},{12,28},{16,0},{20,4},{24,8},{28,12},{1,17},{... | collective-permute-start | bytes 884744 | tf_op jit(solution)/shard_map/ppermute | solution.py:1053
  193.4 43.5 %collective-permute-start.40 = (bf16[96,1536]{1,0:T(8,128)(2,1)S(1)}, bf16[96,1536]{1,0:T(8,128)(2,1)S(1)}, u32[]{:S(2)}, u32[]{:S(2)}) collective-permute-start(bf16[96,1536]{1,0:T(8,128)(2,1)S(1)} %get-tuple-element.165), channel_id=1, source_target_pairs={{0,24},{4,28},{8,0},{12,4},{16,8},{20,12},{24,16},{28,20},{1,25},{... | collective-permute-start | bytes 884744 | tf_op jit(solution)/shard_map/ppermute | solution.py:1053
  238.0 9.5 %collective-permute-start.27 = (bf16[512,768]{1,0:T(8,128)(2,1)S(1)}, bf16[512,768]{1,0:T(8,128)(2,1)S(1)}, u32[]{:S(2)}, u32[]{:S(2)}) collective-permute-start(bf16[512,768]{1,0:T(8,128)(2,1)S(1)} %copy-done.78), channel_id=1, source_target_pairs={{0,1},{1,0},{2,3},{3,2},{4,5},{5,4},{6,7},{7,6},{8,9},{9,8},{10,11... | collective-permute-start | bytes 2359304 | tf_op jit(solution)/shard_map/ppermute | solution.py:1048
  239.5 25.1 %collective-permute-start.44 = (bf16[512,768]{1,0:T(8,128)(2,1)S(1)}, bf16[512,768]{1,0:T(8,128)(2,1)S(1)}, u32[]{:S(2)}, u32[]{:S(2)}) collective-permute-start(bf16[512,768]{1,0:T(8,128)(2,1)S(1)} %add.26.dep), channel_id=1, source_target_pairs={{0,2},{1,3},{2,0},{3,1},{4,6},{5,7},{6,4},{7,5},{8,10},{9,11},{10,... | collective-permute-start | bytes 2359304 | tf_op jit(solution)/shard_map/ppermute | solution.py:1048
  240.0 17.2 %collective-permute-start.45 = (bf16[4,112,576]{2,1,0:T(8,128)(2,1)S(1)}, bf16[4,112,576]{2,1,0:T(8,128)(2,1)S(1)}, u32[]{:S(2)}, u32[]{:S(2)}) collective-permute-start(bf16[4,112,576]{2,1,0:T(8,128)(2,1)S(1)} %get-tuple-element.172), channel_id=1, source_target_pairs={{0,4},{4,0},{8,12},{12,8},{16,20},{20,16},{24,28},{28,24},{1,5},{5... | collective-permute-start | bytes 1548296 | tf_op jit(solution)/shard_map/ppermute | solution.py:1048
  246.1 14.2 %collective-permute-start.42 = (bf16[256,768]{1,0:T(8,128)(2,1)S(1)}, bf16[256,768]{1,0:T(8,128)(2,1)S(1)}, u32[]{:S(2)}, u32[]{:S(2)}) collective-permute-start(bf16[256,768]{1,0:T(8,128)(2,1)S(1)} %get-tuple-element.168), channel_id=1, source_target_pairs={{0,1},{1,0},{2,3},{3,2},{4,5},{5,4},{6,7},{7,6},{8,9},{9,8},{10,11... | collective-permute-start | bytes 1179656 | tf_op jit(solution)/shard_map/ppermute | solution.py:1048
  247.0 16.4 %collective-permute-start.43 = (bf16[256,768]{1,0:T(8,128)(2,1)}, bf16[256,768]{1,0:T(8,128)(2,1)}, u32[]{:S(2)}, u32[]{:S(2)}) collective-permute-start(bf16[256,768]{1,0:T(8,128)(2,1)} %get-tuple-element.169), channel_id=1, source_target_pairs={{0,1},{1,0},{2,3},{3,2},{4,5},{5,4},{6,7},{7,6},{8,9},{9,8},{10,11... | collective-permute-start | bytes 1179656 | tf_op jit(solution)/shard_map/ppermute | solution.py:1048
  258.8 10.4 %collective-permute-start.46 = (bf16[112,576]{1,0:T(8,128)(2,1)}, bf16[112,576]{1,0:T(8,128)(2,1)}, u32[]{:S(2)}, u32[]{:S(2)}) collective-permute-start(bf16[112,576]{1,0:T(8,128)(2,1)} %get-tuple-element.178), channel_id=1, source_target_pairs={{0,8},{4,12},{8,16},{12,20},{16,24},{20,28},{24,0},{28,4},{1,9},{5... | collective-permute-start | bytes 387080 | tf_op jit(solution)/shard_map/ppermute | solution.py:1053
  259.3 12.9 %collective-permute-start.47 = (bf16[112,576]{1,0:T(8,128)(2,1)}, bf16[112,576]{1,0:T(8,128)(2,1)}, u32[]{:S(2)}, u32[]{:S(2)}) collective-permute-start(bf16[112,576]{1,0:T(8,128)(2,1)} %get-tuple-element.179), channel_id=1, source_target_pairs={{0,16},{4,20},{8,24},{12,28},{16,0},{20,4},{24,8},{28,12},{1,17},{... | collective-permute-start | bytes 387080 | tf_op jit(solution)/shard_map/ppermute | solution.py:1053
  260.3 12.0 %collective-permute-start.48 = (bf16[112,576]{1,0:T(8,128)(2,1)}, bf16[112,576]{1,0:T(8,128)(2,1)}, u32[]{:S(2)}, u32[]{:S(2)}) collective-permute-start(bf16[112,576]{1,0:T(8,128)(2,1)} %get-tuple-element.180), channel_id=1, source_target_pairs={{0,24},{4,28},{8,0},{12,4},{16,8},{20,12},{24,16},{28,20},{1,25},{... | collective-permute-start | bytes 387080 | tf_op jit(solution)/shard_map/ppermute | solution.py:1053
  263.4 14.0 %collective-permute-start.52 = (bf16[96,256]{1,0:T(8,128)(2,1)S(1)}, bf16[96,256]{1,0:T(8,128)(2,1)S(1)}, u32[]{:S(2)}, u32[]{:S(2)}) collective-permute-start(bf16[96,256]{1,0:T(8,128)(2,1)S(1)} %slice.4), channel_id=1, source_target_pairs={{0,2},{1,3},{2,0},{3,1},{4,6},{5,7},{6,4},{7,5},{8,10},{9,11},{10,... | collective-permute-start | bytes 147464 | tf_op jit(solution)/shard_map/ppermute | solution.py:1048
  (121 other events, 925.3 us)
Sparse Core Ops, SparseCore 0:
  49.2 49.9 all-gather.1
  185.8 74.1 reduce-scatter.1
